TPU v7x, 32 devices: a whole 2x2x4 slice. The times are simulated.
32 devices in a mesh: dp: 16 (over z, y, core), fsdp: 2 (over x).
Axes of the slice: x: 2, y: 2, z: 4, core: 2. Of those that a mesh axis runs over, the one named last changes fastest.
Arguments:
- pixels: bfloat16 [32768, 640], P(('dp', 'fsdp')), may hold values from -6 to 6
- wave_table: float32 [16], replicated, may hold values from 0.4 to 2.5
- band_count: int32 [7], replicated, may hold values from 3 to 10, as said below
- wave_index: int32 [7, 10], replicated, may hold values from 0 to 15
- group_sensor: int32 [16], replicated, may hold values from 0 to 6
- chip_kind: int32 [32], P(('dp', 'fsdp')), may hold values from 0 to 1
- chip_gsd: int32 [32, 4], P(('dp', 'fsdp')), may hold values from 1 to 30
- time_loc: float32 [32, 4, 8], P(('dp', 'fsdp')), may hold values from -1 to 1
- gen_in: bfloat16 [128, 128], replicated, may hold values from -0.5 to 0.5
- gen_bias: bfloat16 [128], replicated, may hold values from -3 to 3
- gen_out: bfloat16 [128, 49920], P(None, ('dp', 'fsdp')), may hold values from -0.0390625 to 0.0390625
- meta_weight: bfloat16 [9, 768], replicated, may hold values from -3 to 3
- w_qkv: bfloat16 [768, 2304], P('dp', 'fsdp'), may hold values from -0.21875 to 0.21875
- w_out: bfloat16 [768, 768], P('dp', 'fsdp'), may hold values from -0.875 to 0.875
- w_up: bfloat16 [768, 3072], P('dp', 'fsdp'), may hold values from -0.21875 to 0.21875
- w_down: bfloat16 [3072, 768], P('dp', 'fsdp'), may hold values from -0.109375 to 0.109375
- vectors: bfloat16 [768, 6], P('dp')
- b_up: bfloat16 [3072], P('dp'), may hold values from -2 to 2
- cotangent: bfloat16 [33024, 768], P(('dp', 'fsdp')), may hold values from -6 to 6
Outputs:
- layer_out: bfloat16 [33024, 768], P(('dp', 'fsdp'))
- pixel_grad: float32 [32768, 640], P(('dp', 'fsdp'))
- gen_in_grad: float32 [128, 128], replicated
- gen_bias_grad: float32 [128], replicated
- gen_out_grad: float32 [128, 49920], P(None, ('dp', 'fsdp'))
- meta_grad: float32 [9, 768], replicated
- w_qkv_grad: float32 [768, 2304], P('dp', 'fsdp')
- w_out_grad: float32 [768, 768], P('dp', 'fsdp')
- w_up_grad: float32 [768, 3072], P('dp', 'fsdp')
- w_down_grad: float32 [3072, 768], P('dp', 'fsdp')
- vectors_grad: float32 [768, 6], P('dp')
- b_up_grad: float32 [3072], P('dp')
Inputs may be any that keep to these rules, and one draw needn't show every extreme that they name: `band_count`: one sensor has exactly 10 bands.
All inputs are finite; a program needn't handle non-finite values.
Results may differ from a plain program's by a relative error of at most 0.019.
Values may be sent and summed in bfloat16 or wider, within the bound.
A program may use at most 320 MiB of HBM per device.

v0:
```python
import math

import jax
import jax.numpy as jnp
import numpy as np
from jax import lax
from jax.experimental import pallas as pl
from jax.experimental.pallas import tpu as pltpu
from jax.sharding import PartitionSpec as P

D = 768
HEADS = 12
HEAD = 64
GEN = 128
PIX = 64
MAXB = 10
SENSORS = 7
TOK_DEV = 1024
SLOTS = 4
GENOUT = 49920


def exact_dot(left, right):
    return jnp.dot(left, right, precision=lax.Precision.HIGHEST)


def inner_dot(left, right):
    return lax.dot_general(
        left, right, (((0,), (0,)), ((), ())), preferred_element_type=jnp.float32
    )


def outer_dot(left, right):
    return lax.dot_general(
        left, right, (((1,), (1,)), ((), ())), preferred_element_type=jnp.float32
    )


def gelu_exact(values):
    return jax.nn.gelu(values, approximate=False)


def gelu_slope(values, upstream):
    return jax.vjp(gelu_exact, values)[1](upstream)[0]


def table_lookup(indices, table):
    return jnp.sum(
        jnp.where(
            indices[:, None] == jnp.arange(table.shape[0], dtype=jnp.int32)[None, :],
            table[None, :],
            0.0,
        ),
        axis=1,
    )


def wave_code(wavelengths):
    half = GEN // 2
    omega = 1.0 / 10000.0 ** (jnp.arange(half, dtype=jnp.float32) / half)
    angle = (wavelengths * 1000.0)[:, None] * omega[None, :]
    return jnp.concatenate([jnp.sin(angle), jnp.cos(angle)], axis=1)


def place_code(kind_one, gsd_one):
    small = TOK_DEV // SLOTS
    index = jnp.arange(TOK_DEV, dtype=jnp.int32)
    within = jnp.where(kind_one == 1, index, index % small)
    side = jnp.where(kind_one == 1, math.isqrt(TOK_DEV), math.isqrt(small)).astype(jnp.int32)
    across = (within // side).astype(jnp.float32)
    along = (within % side).astype(jnp.float32)
    holder = jnp.where(kind_one == 1, 0, index // small)
    ground = (
        jnp.sum(
            jnp.where(
                holder[:, None] == jnp.arange(SLOTS, dtype=jnp.int32)[None, :], gsd_one[None, :], 0
            ),
            axis=1,
        ).astype(jnp.float32)
        / 10.0
    )
    quarter = D // 4
    omega = 1.0 / 10000.0 ** (jnp.arange(quarter, dtype=jnp.float32) / (quarter - 1))
    first = (across * ground)[:, None] * omega[None, :]
    second = (along * ground)[:, None] * omega[None, :]
    return jnp.concatenate(
        [jnp.sin(first), jnp.cos(first), jnp.sin(second), jnp.cos(second)], axis=1
    )


def segment_ids(kind_one):
    index = jnp.arange(TOK_DEV, dtype=jnp.int32)
    patches = jnp.where(kind_one == 1, 0, index // (TOK_DEV // SLOTS))
    extra = jnp.arange(2 * SLOTS, dtype=jnp.int32) // 2
    return jnp.concatenate([patches, extra])


def layer_norm(values, gain, shift):
    centred = values - jnp.mean(values, axis=-1, keepdims=True)
    scale = lax.rsqrt(jnp.mean(centred * centred, axis=-1, keepdims=True) + 1e-05)
    normed = centred * scale
    return (normed * gain + shift, normed, scale)


def norm_back(upstream, normed, scale, gain):
    gain_grad = jnp.sum(upstream * normed, axis=0)
    shift_grad = jnp.sum(upstream, axis=0)
    scaled = upstream * gain
    inside = (
        scaled
        - jnp.mean(scaled, axis=-1, keepdims=True)
        - normed * jnp.mean(scaled * normed, axis=-1, keepdims=True)
    )
    return (scale * inside, gain_grad, shift_grad)


def body_general(
    pixels,
    wave_table,
    band_count,
    wave_index,
    group_sensor,
    chip_kind,
    chip_gsd,
    time_loc,
    gen_in,
    gen_bias,
    gen_out,
    meta_weight,
    w_qkv,
    w_out,
    w_up,
    w_down,
    vectors,
    b_up,
    cotangent,
):
    half_type = jnp.bfloat16
    group = lax.axis_index("dp")
    sensor = jnp.sum(
        jnp.where(jnp.arange(group_sensor.shape[0], dtype=jnp.int32) == group, group_sensor, 0)
    )
    chosen_sensor = jnp.arange(SENSORS, dtype=jnp.int32) == sensor
    band_total = jnp.sum(jnp.where(chosen_sensor, band_count, 0))
    gen_in_full = gen_in.astype(jnp.float32)
    gen_bias_full = gen_bias.astype(jnp.float32)
    codes = wave_code(table_lookup(wave_index.reshape(-1), wave_table))
    before = exact_dot(codes, gen_in_full) + gen_bias_full
    hidden = gelu_exact(before).astype(half_type)
    shard_made = jnp.dot(hidden, gen_out, preferred_element_type=jnp.float32).astype(half_type)
    all_made = lax.all_gather(shard_made, ("dp", "fsdp"), axis=1, tiled=True)
    generated = lax.dynamic_slice_in_dim(all_made, sensor * MAXB, MAXB, 0)
    live_band = (jnp.arange(MAXB, dtype=jnp.int32) < band_total)[:, None]
    kernel = jnp.where(live_band, generated[:, : PIX * D], jnp.zeros((), half_type)).reshape(
        MAXB * PIX, D
    )
    band_float = band_total.astype(jnp.float32)
    embed_bias = (
        jnp.sum(jnp.where(live_band, generated[:, PIX * D :].astype(jnp.float32), 0.0), axis=0)
        / band_float
    )
    kind_one = chip_kind[0]
    patches = (
        jnp.dot(pixels, kernel, preferred_element_type=jnp.float32)
        + embed_bias
        + place_code(kind_one, chip_gsd[0])
    )
    meta_full = meta_weight.astype(jnp.float32)
    stamps = exact_dot(time_loc[0], meta_full[1:])
    classes = jnp.broadcast_to(meta_full[0], stamps.shape)
    extra = jnp.stack([classes, stamps], axis=1).reshape(2 * SLOTS, D)
    tokens_in = jnp.concatenate([patches, extra], axis=0)
    total_rows = tokens_in.shape[0]
    qkv_rows, out_rows, up_rows, down_rows, vectors_all, b_up_all = (
        lax.all_gather(w_qkv, "dp", axis=0, tiled=True),
        lax.all_gather(w_out, "dp", axis=0, tiled=True),
        lax.all_gather(w_up, "dp", axis=0, tiled=True),
        lax.all_gather(w_down, "dp", axis=0, tiled=True),
        lax.all_gather(vectors, "dp", axis=0, tiled=True),
        lax.all_gather(b_up, "dp", axis=0, tiled=True),
    )
    w_qkv_all, w_out_all, w_up_all, w_down_all = (
        lax.all_gather(qkv_rows, "fsdp", axis=1, tiled=True),
        lax.all_gather(out_rows, "fsdp", axis=1, tiled=True),
        lax.all_gather(up_rows, "fsdp", axis=1, tiled=True),
        lax.all_gather(down_rows, "fsdp", axis=1, tiled=True),
    )
    vector_full = vectors_all.astype(jnp.float32)
    b_up_full = b_up_all.astype(jnp.float32)
    first_norm, normed_one, scale_one = layer_norm(tokens_in, vector_full[:, 0], vector_full[:, 1])
    first = first_norm.astype(half_type)
    qkv = jnp.dot(first, w_qkv_all, preferred_element_type=jnp.float32).astype(half_type)
    query = qkv[:, :D].reshape(total_rows, HEADS, HEAD)
    keys = qkv[:, D : 2 * D].reshape(total_rows, HEADS, HEAD)
    values = qkv[:, 2 * D :].reshape(total_rows, HEADS, HEAD)
    segment = segment_ids(kind_one)
    same = (segment[:, None] == segment[None, :])[None]
    scores = jnp.einsum("qhd,khd->hqk", query, keys, preferred_element_type=jnp.float32) * HEAD ** (
        -0.5
    )
    scores = jnp.where(same, scores, -1e30)
    peak = jnp.max(scores, axis=-1, keepdims=True)
    expo = jnp.exp(scores - peak)
    totals = jnp.sum(expo, axis=-1, keepdims=True)
    prob_half = (expo / totals).astype(half_type)
    mixed = (
        jnp.einsum("hqk,khd->qhd", prob_half, values, preferred_element_type=jnp.float32)
        .reshape(total_rows, D)
        .astype(half_type)
    )
    after = tokens_in + (
        jnp.dot(mixed, w_out_all, preferred_element_type=jnp.float32) + vector_full[:, 2]
    )
    second_norm, normed_two, scale_two = layer_norm(after, vector_full[:, 3], vector_full[:, 4])
    second = second_norm.astype(half_type)
    upper = jnp.dot(second, w_up_all, preferred_element_type=jnp.float32) + b_up_full
    active = gelu_exact(upper).astype(half_type)
    layer_out = (
        after + jnp.dot(active, w_down_all, preferred_element_type=jnp.float32) + vector_full[:, 5]
    ).astype(half_type)
    grad_top = cotangent.astype(jnp.float32)
    w_down_grad = inner_dot(active, cotangent)
    down_bias_grad = jnp.sum(grad_top, axis=0)
    d_active = outer_dot(cotangent, w_down_all)
    d_upper = gelu_slope(upper, d_active).astype(half_type)
    w_up_grad = inner_dot(second, d_upper)
    b_up_grad = jnp.sum(d_upper.astype(jnp.float32), axis=0)
    d_second = outer_dot(d_upper, w_up_all)
    d_after_norm, gain_two_grad, shift_two_grad = norm_back(
        d_second, normed_two, scale_two, vector_full[:, 3]
    )
    d_after = grad_top + d_after_norm
    d_proj = d_after.astype(half_type)
    w_out_grad = inner_dot(mixed, d_proj)
    out_bias_grad = jnp.sum(d_proj.astype(jnp.float32), axis=0)
    d_mixed = outer_dot(d_proj, w_out_all).astype(half_type).reshape(total_rows, HEADS, HEAD)
    again = jnp.einsum("qhd,khd->hqk", query, keys, preferred_element_type=jnp.float32) * HEAD ** (
        -0.5
    )
    again = jnp.where(same, again, -1e30)
    prob_full = jnp.exp(again - peak) / totals
    recalled = prob_full.astype(half_type)
    d_values = jnp.einsum("hqk,qhd->khd", recalled, d_mixed, preferred_element_type=jnp.float32)
    d_prob = jnp.einsum("qhd,khd->hqk", d_mixed, values, preferred_element_type=jnp.float32)
    d_scores = prob_full * (d_prob - jnp.sum(d_prob * prob_full, axis=-1, keepdims=True))
    d_scores = jnp.where(same, d_scores, 0.0).astype(half_type)
    d_query = jnp.einsum(
        "hqk,khd->qhd", d_scores, keys, preferred_element_type=jnp.float32
    ) * HEAD ** (-0.5)
    d_keys = jnp.einsum(
        "hqk,qhd->khd", d_scores, query, preferred_element_type=jnp.float32
    ) * HEAD ** (-0.5)
    d_qkv = jnp.concatenate(
        [
            d_query.reshape(total_rows, D),
            d_keys.reshape(total_rows, D),
            d_values.reshape(total_rows, D),
        ],
        axis=1,
    ).astype(half_type)
    w_qkv_grad = inner_dot(first, d_qkv)
    d_first = outer_dot(d_qkv, w_qkv_all)
    d_tokens_norm, gain_one_grad, shift_one_grad = norm_back(
        d_first, normed_one, scale_one, vector_full[:, 0]
    )
    d_tokens = (d_after + d_tokens_norm).astype(half_type)
    vectors_grad = jnp.stack(
        [
            gain_one_grad,
            shift_one_grad,
            out_bias_grad,
            gain_two_grad,
            shift_two_grad,
            down_bias_grad,
        ],
        axis=1,
    )
    d_patches = d_tokens[:TOK_DEV]
    d_extra = d_tokens[TOK_DEV:].astype(jnp.float32).reshape(SLOTS, 2, D)
    pixel_grad = outer_dot(d_patches, kernel)
    class_grad = jnp.sum(d_extra[:, 0], axis=0)
    stamp_grad = exact_dot(time_loc[0].T, d_extra[:, 1])
    meta_part = jnp.concatenate([class_grad[None, :], stamp_grad], axis=0)
    d_kernel = inner_dot(pixels, d_patches).reshape(MAXB, PIX * D)
    d_kernel = jnp.where(live_band, d_kernel, 0.0)
    d_bias = jnp.sum(d_patches.astype(jnp.float32), axis=0) / band_float
    d_bias_rows = jnp.where(live_band, d_bias[None, :], 0.0)
    d_generated = jnp.concatenate([d_kernel, d_bias_rows], axis=1).astype(half_type)
    placed = jnp.where(
        chosen_sensor[:, None, None], d_generated.astype(jnp.float32)[None], 0.0
    ).reshape(SENSORS * MAXB, GENOUT)
    columns = lax.psum_scatter(placed, ("dp", "fsdp"), scatter_dimension=1, tiled=True)
    gen_out_grad = exact_dot(hidden.astype(jnp.float32).T, columns)
    d_hidden = exact_dot(columns, gen_out.astype(jnp.float32).T)
    d_before = gelu_slope(before, d_hidden)
    gen_in_part = exact_dot(codes.T, d_before)
    gen_bias_part = jnp.sum(d_before, axis=0)
    meta_grad, gen_in_grad, gen_bias_grad = lax.psum(
        (meta_part, gen_in_part, gen_bias_part), ("dp", "fsdp")
    )
    qkv_cols, out_cols, up_cols, down_cols = (
        lax.psum_scatter(
            w_qkv_grad.astype(jnp.bfloat16), "fsdp", scatter_dimension=1, tiled=True
        ).astype(jnp.float32),
        lax.psum_scatter(
            w_out_grad.astype(jnp.bfloat16), "fsdp", scatter_dimension=1, tiled=True
        ).astype(jnp.float32),
        lax.psum_scatter(
            w_up_grad.astype(jnp.bfloat16), "fsdp", scatter_dimension=1, tiled=True
        ).astype(jnp.float32),
        lax.psum_scatter(
            w_down_grad.astype(jnp.bfloat16), "fsdp", scatter_dimension=1, tiled=True
        ).astype(jnp.float32),
    )
    vectors_group, b_up_group = lax.psum((vectors_grad, b_up_grad), "fsdp")
    w_qkv_out, w_out_out, w_up_out, w_down_out, vectors_out, b_up_out = (
        lax.psum_scatter(
            qkv_cols.astype(jnp.bfloat16), "dp", scatter_dimension=0, tiled=True
        ).astype(jnp.float32),
        lax.psum_scatter(
            out_cols.astype(jnp.bfloat16), "dp", scatter_dimension=0, tiled=True
        ).astype(jnp.float32),
        lax.psum_scatter(
            up_cols.astype(jnp.bfloat16), "dp", scatter_dimension=0, tiled=True
        ).astype(jnp.float32),
        lax.psum_scatter(
            down_cols.astype(jnp.bfloat16), "dp", scatter_dimension=0, tiled=True
        ).astype(jnp.float32),
        lax.psum_scatter(
            vectors_group.astype(jnp.bfloat16), "dp", scatter_dimension=0, tiled=True
        ).astype(jnp.float32),
        lax.psum_scatter(
            b_up_group.astype(jnp.bfloat16), "dp", scatter_dimension=0, tiled=True
        ).astype(jnp.float32),
    )
    return (
        layer_out,
        pixel_grad,
        gen_in_grad,
        gen_bias_grad,
        gen_out_grad,
        meta_grad,
        w_qkv_out,
        w_out_out,
        w_up_out,
        w_down_out,
        vectors_out,
        b_up_out,
    )


LIVE = 1032
ROWS = 1040
TILE = 208
TILES = 5
NZ = 4
GROUPS = 16
PIECE = 144
COVER = 14
VMEM_ASK = 60 * 1024 * 1024
BF = jnp.bfloat16
F32 = jnp.float32


def nt_dot(left, right):
    return lax.dot_general(left, right, (((1,), (1,)), ((), ())), preferred_element_type=F32)


def nn_dot(left, right):
    return lax.dot_general(left, right, (((1,), (0,)), ((), ())), preferred_element_type=F32)


def spot():
    group = lax.axis_index("dp")
    return group // 4, (group // 2) % 2, group % 2, lax.axis_index("fsdp")


def device(z, y, c, x):
    return {"dp": z * 4 + y * 2 + c, "fsdp": x}


def remote(source, target, sems, slot, where):
    return pltpu.make_async_remote_copy(
        src_ref=source,
        dst_ref=target,
        send_sem=sems[0].at[slot],
        recv_sem=sems[1].at[slot],
        device_id=where,
        device_id_type=pl.DeviceIdType.MESH,
    )


def greet(others):
    barrier = pltpu.get_barrier_semaphore()
    for where in others:
        pl.semaphore_signal(
            barrier, inc=1, device_id=where, device_id_type=pl.DeviceIdType.MESH
        )
    pl.semaphore_wait(barrier, len(others))


def columns(ref, x):
    width = ref.shape[-1] // 2
    return pl.ds(pl.multiple_of(x * width, 128), width)


def group_peers(z, y, c, x):
    return [
        ((dz, dy, dc), device((z + dz) % NZ, (y + dy) % 2, (c + dc) % 2, x))
        for dz in range(NZ)
        for dy in range(2)
        for dc in range(2)
        if dz + dy + dc
    ]


CHUNK = 768
BANDS = ((0, 256), (256, 256), (512, 256), (768, 256), (1024, 8))


def gelu_parts(values):
    bell = jnp.exp(values * values * (-0.5))
    step = 1.0 / (1.0 + (0.3275911 * math.sqrt(0.5)) * jnp.abs(values))
    poly = 0.5 * 1.061405429 * step - 0.5 * 1.453152027
    poly = poly * step + 0.5 * 1.421413741
    poly = poly * step - 0.5 * 0.284496736
    poly = poly * step + 0.5 * 0.254829592
    tail = poly * step * bell
    below = jnp.where(values < 0.0, tail, 1.0 - tail)
    return values * below, below + values * bell * (1.0 / math.sqrt(2.0 * math.pi))


def standard(values):
    centred = values - jnp.mean(values, axis=-1, keepdims=True)
    scale = lax.rsqrt(jnp.mean(centred * centred, axis=-1, keepdims=True) + 1e-05)
    return centred * scale, scale


def column_sum(values):
    return jnp.sum(values, axis=0, keepdims=True)


def put_rows(target, first, count, values):
    if count % 16:
        values = jnp.concatenate(
            [values, jnp.zeros((16 - count % 16, values.shape[1]), values.dtype)], axis=0
        )
    target[first : first + values.shape[0], :] = values


class Gather:
    COPIES = 19

    def __init__(self, shard, whole, sems, local, first, lean, here):
        z, y, c, x = here
        self.lean = lean
        mine, other = columns(whole, x), columns(whole, 1 - x)
        across, beside, twin = device(z, y, c, 1 - x), device(z, 1 - y, c, x), device(z, y, 1 - c, x)
        target = whole.at[z, y, c, :, mine]
        self.local = pltpu.make_async_copy(shard, target, local)
        self.along = [
            remote(shard, target, sems, first + k - 1, device((z + k) % NZ, y, c, x))
            for k in range(1, NZ)
        ]
        self.to_x, self.to_y, self.far = [], [], []
        for k in range(NZ):
            at = (z + NZ - k) % NZ
            place = whole.at[at, y, c, :, mine]
            source = place if k else shard
            self.to_x.append(remote(source, place, sems, first + 3 + k, across))
            self.to_y.append(remote(source, place, sems, first + 7 + k, beside))
            if k < lean:
                place = whole.at[at, y, c, :, other]
                self.far.append(remote(place, place, sems, first + 11 + k, beside))
            else:
                place = whole.at[at, 1 - y, c, :, mine]
                self.far.append(remote(place, place, sems, first + 11 + k, across))
        self.core = []
        for step, part in enumerate(
            (
                whole.at[:, y, c, :, mine],
                whole.at[:, y, c, :, other],
                whole.at[:, 1 - y, c, :, mine],
                whole.at[:, 1 - y, c, :, other],
            )
        ):
            self.core.append(remote(part, part, sems, first + 15 + step, twin))

    def send_z(self):
        self.local.start()
        for copy in self.along:
            copy.start()

    def send_own(self):
        self.to_x[0].start()
        self.to_y[0].start()

    def pass_on(self):
        for k in range(1, NZ):
            self.along[k - 1].wait_recv()
            self.to_x[k].start()
            self.to_y[k].start()
        self.local.wait()
        self.core[0].start()

    def turn_corner(self):
        for k in range(NZ):
            (self.to_x if k < self.lean else self.to_y)[k].wait_recv()
            self.far[k].start()
        for k in range(self.lean, NZ):
            self.to_x[k].wait_recv()
        self.core[1].start()
        for k in range(self.lean):
            self.to_y[k].wait_recv()
        self.core[2].start()

    def share(self):
        for copy in self.far:
            copy.wait_recv()
        self.core[3].start()

    def receive(self):
        for copy in self.core:
            copy.wait_recv()

    def finish(self):
        for copy in (*self.along, *self.to_x, *self.to_y, *self.far, *self.core):
            copy.wait_send()


def make_small(vectors, b_up, held, small):
    group = lax.axis_index("dp")
    count, up_count = vectors.shape[1], b_up.shape[1]
    per_row = D // up_count
    held[...] = jnp.zeros_like(held)
    held[0:6, 0:count] = vectors[...].astype(F32)
    held[8:9, 0:up_count] = b_up[...].astype(F32)
    rows = pltpu.roll(held[0:8, :], group * count, 1)
    bias = pltpu.roll(held[8:16, :], (group % per_row) * up_count, 1)[0:1]
    row = lax.broadcasted_iota(jnp.int32, (8, D), 0)
    spot_at = 6 + group // per_row
    top = jnp.where(row < 6, rows, jnp.where(row == spot_at, bias, 0.0))
    small[...] = jnp.concatenate(
        [top, jnp.where(row + 8 == spot_at, bias, 0.0)], axis=0
    ).astype(BF)


def make_table(kind, ground, steps, table):
    wide = steps.shape[1]
    entry = lax.broadcasted_iota(jnp.int32, (64, wide), 0)
    lane = lax.broadcasted_iota(jnp.int32, (64, wide), 1)
    single = kind == 1
    chip = jnp.where(single, 0, entry // 16)
    step = jnp.where(single, entry, entry % 16).astype(F32)
    distance = jnp.zeros((64, wide), F32)
    for slot in range(SLOTS):
        distance = jnp.where(chip == slot, ground[0, slot].astype(F32), distance)
    angle = (step * (distance / 10.0)) * steps[0:1, :]
    exact = jnp.where(lane < wide // 2, jnp.sin(angle), jnp.cos(angle))
    for at, part in enumerate(three_parts(exact)):
        table[at * 64 : (at + 1) * 64, :] = part
    table[192:256, :] = jnp.zeros((64, wide), BF)


def make_pieces(
    groups, bands, waves, wave_table, steps, gen_in, gen_bias, gen_out,
    gen_shift, hidden, slope, codes, made, code_rows, rows, wide, angles,
):
    for wave in range(angles.shape[0]):
        angles[wave : wave + 1, :] = (wave_table[wave] * 1000.0) * steps[0:1, :]
    lane = lax.broadcasted_iota(jnp.int32, angles.shape, 1)
    angle = angles[...]
    angles[...] = jnp.where(lane < GEN // 2, jnp.sin(angle), jnp.cos(angle))
    for sensor in range(SENSORS):
        for band in range(MAXB):
            code_rows[sensor, band : band + 1, :] = angles[pl.ds(waves[sensor, band], 1), :]
        code_rows[sensor, MAXB:16, :] = jnp.zeros((16 - MAXB, GEN), F32)
    flat = code_rows[:, 0:16, :].reshape(SENSORS * 16, GEN)
    before = exact_dot(flat, gen_in[...].astype(F32)) + gen_bias[...].astype(F32)
    values, slopes = gelu_parts(before)
    band_at = lax.broadcasted_iota(jnp.int32, (16, GEN), 0)
    width = gen_out.shape[0]
    owner = lax.axis_index("dp") * 2 + lax.axis_index("fsdp")
    wide[...] = jnp.zeros_like(wide)
    wide[pl.ds(pl.multiple_of((owner * width) % 128, 8), width), :] = gen_out[...].astype(F32)
    gen_shift[...] = wide[...].astype(BF)
    kept = []
    for sensor in range(SENSORS):
        part = slice(sensor * 16, sensor * 16 + 16)
        live = band_at < bands[sensor]
        kept.append(jnp.where(live, values[part], 0.0))
        code_rows[sensor, 16:32, :] = kept[-1].astype(BF).astype(F32)
        code_rows[sensor, 32:48, :] = jnp.where(live, slopes[part], 0.0)
    lower = jnp.concatenate(kept, axis=0).astype(BF)
    for at in range(COVER):
        product = nt_dot(lower, gen_shift[at * 128 : (at + 1) * 128, :])
        for sensor in range(SENSORS):
            rows[sensor, at * MAXB : (at + 1) * MAXB, :] = product[
                sensor * 16 : sensor * 16 + MAXB
            ]
    rows[:, COVER * MAXB :, :] = jnp.zeros((SENSORS, PIECE - COVER * MAXB, 128), F32)
    for group in range(GROUPS):
        made[group // 4, (group // 2) % 2, group % 2] = rows[groups[group]].astype(BF)
    for group in range(GROUPS):
        own = code_rows[groups[group]]
        first = group * MAXB
        codes[first : first + MAXB, :] = own[0:MAXB]
        hidden[first : first + MAXB, :] = own[16 : 16 + MAXB]
        slope[first : first + MAXB, :] = own[32 : 32 + MAXB]


def mask_rows(kind, for_query, for_key):
    row = lax.broadcasted_iota(jnp.int32, (ROWS, 128), 0)
    lane = lax.broadcasted_iota(jnp.int32, (ROWS, 128), 1)
    patch = jnp.where(kind == 1, 0, row // (TOK_DEV // SLOTS))
    segment = jnp.where(row < TOK_DEV, patch, (row - TOK_DEV) // 2)
    hot = (lane == segment) & (row < LIVE)
    for_query[...] = jnp.where(hot, 1.0, 0.0).astype(BF)
    for_key[...] = jnp.where(
        lane < SLOTS, jnp.where(hot, 0.0, -1e30), jnp.where(lane < SLOTS + 3, 1.0, 0.0)
    ).astype(BF)


def attend_pair(pair, qkv, mask_q, mask_k, keys, values, mixed, log_sum):
    lane = lax.broadcasted_iota(jnp.int32, (TILE, 128), 1)
    lanes = pl.ds(pl.multiple_of(pair * 128, 128), 128)
    keys[:, 0:128] = qkv[6 + pair]
    keys[:, 128:256] = mask_k[...]
    values[:, 0:128] = qkv[12 + pair]
    for tile in range(TILES):
        first = tile * TILE
        both = qkv[pair, first : first + TILE, :] * BF(0.125)
        results, sums = [], []
        for head in range(2):
            query = jnp.where((lane < HEAD) == (head == 0), both, BF(0))
            scores = nt_dot(
                jnp.concatenate([query, mask_q[first : first + TILE, :]], axis=1), keys[...]
            )
            peak = jnp.max(scores, axis=1, keepdims=True)
            expo = jnp.exp(scores - peak).astype(BF)
            made = nn_dot(expo, values[...])
            totals = made[:, 128:256]
            results.append(made[:, 0:128] / totals)
            sums.append(peak + jnp.log(totals))
        count = min(TILE, LIVE - first)
        mixed[first : first + count, lanes] = jnp.where(lane < HEAD, *results)[:count].astype(BF)
        log_sum[pair, first : first + TILE, :] = jnp.where(lane < HEAD, *sums)


def forward_kernel(
    wq, wo, wu, wd, pixels, vectors, b_up, meta_weight, time_loc, gen_in, gen_bias, gen_out,
    wave_steps, place_steps,
    groups, bands, waves, wave_table, kind, ground,
    full_q, full_o, full_u, full_d, params, kernel, tokens, first, qkv, mixed, log_sum,
    gen_shift, hidden, slope, codes,
    made, code_rows, rows, roll, angles, small_held, small, table,
    taken, full_small, flat, wide, keys, values, mask_q, mask_k,
    w_send, w_recv, local_sem, s_send, s_recv, g_send, g_recv,
):
    here = z, y, c, x = spot()
    peers = group_peers(z, y, c, x)
    across = device(z, y, c, 1 - x)
    greet([where for _, where in peers] + [across])
    gathers = q, o, u, d = [
        Gather(shard, whole, (w_send, w_recv), local_sem.at[step], Gather.COPIES * step, lean, here)
        for step, (shard, whole, lean) in enumerate(
            ((wq, full_q, 3), (wo, full_o, 2), (wu, full_u, 3), (wd, full_d, 2))
        )
    ]
    s_sems = (s_send, s_recv)
    g_sems = (g_send, g_recv)
    q.send_z()
    for gather in gathers:
        gather.send_own()
    make_pieces(
        groups, bands, waves, wave_table, wave_steps, gen_in, gen_bias, gen_out,
        gen_shift, hidden, slope, codes, made, code_rows, rows, roll, angles,
    )
    make_small(vectors, b_up, small_held, small)
    mask_rows(kind[0], mask_q, mask_k)
    make_table(kind[0], ground, place_steps, table)
    values[:, 128:256] = jnp.ones((ROWS, 128), BF)
    q.pass_on()
    own_made = pltpu.make_async_copy(
        made.at[z, y, c], taken.at[z, y, c, x], local_sem.at[4]
    )
    own_made.start()
    sends = {}
    for (dz, dy, dc), where in peers:
        copy = remote(
            made.at[(z + dz) % NZ, (y + dy) % 2, (c + dc) % 2],
            taken.at[z, y, c, x],
            g_sems,
            dz * 4 + dy * 2 + dc,
            where,
        )
        copy.start()
        sends[dz, dy, dc] = copy
    own_small = pltpu.make_async_copy(small, full_small.at[z, y, c], local_sem.at[5])
    own_small.start()
    small_z = [
        remote(small, full_small.at[z, y, c], s_sems, k - 1, device((z + k) % NZ, y, c, x))
        for k in range(1, NZ)
    ]
    for copy in small_z:
        copy.start()
    q.turn_corner()
    own_made.wait()
    swaps = []
    for dz in range(NZ):
        for dy in range(2):
            for dc in range(2):
                if dz + dy + dc:
                    sends[dz, dy, dc].wait_recv()
        part = taken.at[(z + NZ - dz) % NZ, :, :, x]
        swap = remote(part, part, g_sems, 16 + dz, across)
        swap.start()
        swaps.append(swap)
    u.send_z()
    own_small.wait()
    for copy in small_z:
        copy.wait_recv()
    part = full_small.at[:, y, c]
    small_y = remote(part, part, s_sems, 3, device(z, 1 - y, c, x))
    small_y.start()
    q.share()
    for swap in swaps:
        swap.wait_recv()
    small_y.wait_recv()
    part = full_small.at[:, :, c]
    small_c = remote(part, part, s_sems, 4, device(z, y, 1 - c, x))
    small_c.start()
    unpack(taken, flat, wide, kernel)
    bias = jnp.concatenate(
        [
            column_sum(flat[(PIX * 6 + part) * MAXB : (PIX * 6 + part + 1) * MAXB, :])
            for part in range(6)
        ],
        axis=1,
    ) / bands[groups[lax.axis_index("dp")]].astype(F32)
    single = kind[0] == 1
    for start, count in BANDS[:-1]:
        band = slice(start, start + count)
        made_rows = nn_dot(pixels[band, :], kernel[...])
        index = start + lax.broadcasted_iota(jnp.int32, (count, 256), 0)
        lane = lax.broadcasted_iota(jnp.int32, (count, 256), 1)
        spread = []
        for spots in (
            jnp.where(single, index // 32, index // 16),
            jnp.where(single, index % 32, index // 256 * 16 + index % 16),
        ):
            hot = (lane % 64 == spots) & (lane < 192)
            spread.append(nn_dot(jnp.where(hot, 1.0, 0.0).astype(BF), table[...]))
        tokens[band, :] = made_rows + bias + jnp.concatenate(spread, axis=1)
    u.pass_on()
    d.send_z()
    small_c.wait_recv()
    params[...] = jnp.zeros_like(params)
    for n in range(GROUPS):
        params[...] += full_small[n // 4, (n // 2) % 2, n % 2].astype(F32)
    meta = meta_weight[...].astype(F32)
    stamps = exact_dot(time_loc[0], meta[1:])
    for slot in range(SLOTS):
        at = TOK_DEV + 2 * slot
        tokens[at : at + 1, :] = meta[0:1]
        tokens[at + 1 : at + 2, :] = stamps[slot : slot + 1]
    for start, count in BANDS:
        band = slice(start, start + count)
        normed, _ = standard(tokens[band, :])
        first[band, :] = (normed * params[0:1, :] + params[1:2, :]).astype(BF)
    q.receive()
    for start, count in BANDS:
        band = slice(start, start + count)
        for third in range(3):
            part = slice(third * D, (third + 1) * D)
            made_rows = nn_dot(
                first[band, :], full_q[:, :, :, :, part].reshape(D, D)
            ).astype(BF)
            for block in range(6):
                put_rows(
                    qkv.at[third * 6 + block],
                    start,
                    count,
                    made_rows[:, block * 128 : (block + 1) * 128],
                )

    def one_pair(pair, carry):
        @pl.when(pair == 1)
        def _():
            d.pass_on()
            o.send_z()
            u.turn_corner()

        @pl.when(pair == 2)
        def _():
            o.pass_on()

        @pl.when(pair == 3)
        def _():
            d.turn_corner()
            u.share()

        @pl.when(pair == 4)
        def _():
            o.turn_corner()
            d.share()

        @pl.when(pair == 5)
        def _():
            o.share()

        attend_pair(pair, qkv, mask_q, mask_k, keys, values, mixed, log_sum)
        return carry

    lax.fori_loop(0, HEADS // 2, one_pair, 0)
    for gather in (o, u, d):
        gather.receive()
    for gather in gathers:
        gather.finish()
    for copy in (*small_z, small_y, small_c, *sends.values(), *swaps):
        copy.wait_send()


def forward(shards, operands, scalars):
    anywhere = pl.BlockSpec(memory_space=pl.ANY)
    vmem = pl.BlockSpec(memory_space=pltpu.VMEM)
    smem = pl.BlockSpec(memory_space=pltpu.SMEM)
    blocks = GROUPS * MAXB
    outs = [
        jax.ShapeDtypeStruct((NZ, 2, 2, shard.shape[0], 2 * shard.shape[1]), BF) for shard in shards
    ]
    outs += [
        jax.ShapeDtypeStruct((16, D), F32),
        jax.ShapeDtypeStruct((MAXB * PIX, D), BF),
        jax.ShapeDtypeStruct((LIVE, D), F32),
        jax.ShapeDtypeStruct((LIVE, D), BF),
        jax.ShapeDtypeStruct((18, ROWS, 128), BF),
        jax.ShapeDtypeStruct((LIVE, D), BF),
        jax.ShapeDtypeStruct((HEADS // 2, ROWS, 128), F32),
        jax.ShapeDtypeStruct((COVER * 128, GEN), BF),
        jax.ShapeDtypeStruct((blocks, GEN), F32),
        jax.ShapeDtypeStruct((blocks, GEN), F32),
        jax.ShapeDtypeStruct((blocks, GEN), F32),
    ]
    return pl.pallas_call(
        forward_kernel,
        out_shape=outs,
        in_specs=[anywhere] * 4 + [vmem] * len(operands) + [smem] * len(scalars),
        out_specs=[vmem] + [anywhere] * 3 + [vmem] * 11,
        scratch_shapes=[
            pltpu.VMEM((NZ, 2, 2, PIECE, 128), BF),
            pltpu.VMEM((SENSORS, 48, GEN), F32),
            pltpu.VMEM((SENSORS, PIECE, 128), F32),
            pltpu.VMEM((COVER * 128, GEN), F32),
            pltpu.VMEM((scalars[3].shape[0], GEN), F32),
            pltpu.VMEM((16, D), F32),
            pltpu.VMEM((16, D), BF),
            pltpu.VMEM((256, D // 2), BF),
            pltpu.VMEM((NZ, 2, 2, 2, PIECE, 128), BF),
            pltpu.VMEM((NZ, 2, 2, 16, D), BF),
            pltpu.VMEM((FLAT, 128), F32),
            pltpu.VMEM((6, MAXB * PIX, 128), F32),
            pltpu.VMEM((ROWS, 256), BF),
            pltpu.VMEM((ROWS, 256), BF),
            pltpu.VMEM((ROWS, 128), BF),
            pltpu.VMEM((ROWS, 128), BF),
        ]
        + [pltpu.SemaphoreType.DMA((count,)) for count in (76, 76, 6, 5, 5, 20, 20)],
        compiler_params=pltpu.CompilerParams(
            collective_id=0, has_side_effects=True, vmem_limit_bytes=VMEM_ASK
        ),
    )(*shards, *operands, *scalars)


class Scatter:
    def __init__(self, whole, own, came, low, high, side_x, side_y, last, out, sems, first, here):
        z, y, c, x = here
        self.here, self.own, self.came, self.out = here, own, came, out
        self.low, self.high, self.side_x, self.side_y, self.last = low, high, side_x, side_y, last
        self.mine, self.other = columns(own, x), columns(own, 1 - x)
        mine, other = self.mine, self.other
        across, beside, twin = device(z, y, c, 1 - x), device(z, 1 - y, c, x), device(z, y, 1 - c, x)
        self.local = pltpu.make_async_copy(whole.at[:, :, c], own, sems[2].at[first // 8])
        self.core = remote(whole.at[:, :, 1 - c], came, sems, first, twin)
        self.far_y = remote(own.at[0:2, 1 - y, :, other], low, sems, first + 1, beside)
        self.far_x = remote(own.at[2:4, 1 - y, :, other], high, sems, first + 2, across)
        self.to_x = remote(own.at[:, y, :, other], side_x, sems, first + 3, across)
        self.to_y = remote(own.at[:, 1 - y, :, mine], side_y, sems, first + 4, beside)
        self.along = [
            remote(
                own.at[(z + k) % NZ, y, :, mine], last.at[k - 1], sems, first + 4 + k,
                device((z + k) % NZ, y, c, x),
            )
            for k in range(1, NZ)
        ]

    def stage_a(self):
        self.local.start()
        self.core.start()

    def stage_b(self):
        self.local.wait()
        self.core.wait_recv()
        for at_z in range(NZ):
            for at_y in range(2):
                self.own[at_z, at_y] = (
                    self.own[at_z, at_y].astype(F32) + self.came[at_z, at_y].astype(F32)
                ).astype(BF)
        self.far_y.start()
        self.far_x.start()

    def stage_c(self):
        _, y, _, _ = self.here
        self.far_y.wait_recv()
        for k in range(2):
            self.own[k, y, :, self.other] = (
                self.own[k, y, :, self.other].astype(F32) + self.low[k].astype(F32)
            ).astype(BF)
        self.to_x.start()
        self.far_x.wait_recv()
        for k in range(2):
            self.own[2 + k, 1 - y, :, self.mine] = (
                self.own[2 + k, 1 - y, :, self.mine].astype(F32) + self.high[k].astype(F32)
            ).astype(BF)
        self.to_y.start()

    def stage_d(self):
        _, y, _, _ = self.here
        self.to_x.wait_recv()
        self.to_y.wait_recv()
        for k in range(NZ):
            self.own[k, y, :, self.mine] = (
                self.own[k, y, :, self.mine].astype(F32)
                + self.side_x[k].astype(F32)
                + self.side_y[k].astype(F32)
            ).astype(BF)
        for copy in self.along:
            copy.start()

    def stage_e(self):
        z, y, _, _ = self.here
        for copy in self.along:
            copy.wait_recv()
        self.out[...] = (
            self.own[z, y, :, self.mine].astype(F32)
            + self.last[0].astype(F32)
            + self.last[1].astype(F32)
            + self.last[2].astype(F32)
        )
        for copy in (self.core, self.far_y, self.far_x, self.to_x, self.to_y, *self.along):
            copy.wait_send()


class Total:
    COPIES = 7

    def __init__(self, source, out, held, came, slots, send_sem, recv_sem, here):
        z, y, c, x = here
        sems = (send_sem, recv_sem)
        half = source.shape[0] // 2
        self.mine = pl.ds(pl.multiple_of(c * half, 8), half)
        theirs = pl.ds(pl.multiple_of((1 - c) * half, 8), half)
        self.source, self.held, self.came, self.slots, self.out = source, held, came, slots, out
        self.z = z
        twin = device(z, y, 1 - c, x)
        self.steps = [
            remote(source.at[theirs], came.at[0], sems, 0, twin),
            remote(held.at[0], came.at[1], sems, 1, device(z, y, c, 1 - x)),
            remote(held.at[1], came.at[2], sems, 2, device(z, 1 - y, c, x)),
        ]
        self.along = [
            remote(held.at[2], slots.at[z], sems, 2 + k, device((z + k) % NZ, y, c, x))
            for k in range(1, NZ)
        ]
        self.last = remote(out.at[self.mine], out.at[self.mine], sems, 6, twin)

    def begin(self):
        self.steps[0].start()

    def turn(self, step):
        self.steps[step].wait_recv()
        before = self.source[self.mine, :] if step == 0 else self.held[step - 1]
        self.held[step] = before + self.came[step]
        if step < 2:
            self.steps[step + 1].start()
        else:
            self.slots[self.z] = self.held[2]
            for copy in self.along:
                copy.start()

    def close(self):
        for copy in self.along:
            copy.wait_recv()
        self.out[self.mine, :] = self.slots[0] + self.slots[1] + self.slots[2] + self.slots[3]
        self.last.start()

    def finish(self):
        for copy in (*self.steps, *self.along):
            copy.wait_send()
        self.last.wait()


def near(z, y, c, x):
    return [
        device(z, y, c, 1 - x),
        device(z, 1 - y, c, x),
        device(z, y, 1 - c, x),
        *[device((z + k) % NZ, y, c, x) for k in range(1, NZ)],
    ]


def scatter_scratch(rows, width):
    half = width // 2
    return [
        pltpu.VMEM((NZ, 2, rows, width), BF),
        pltpu.VMEM((NZ, 2, rows, width), BF),
        pltpu.VMEM((2, rows, half), BF),
        pltpu.VMEM((2, rows, half), BF),
        pltpu.VMEM((NZ, rows, half), BF),
        pltpu.VMEM((NZ, rows, half), BF),
        pltpu.VMEM((3, rows, half), BF),
    ]


def total_scratch(shape):
    half = (shape[0] // 2,) + shape[1:]
    return [
        pltpu.VMEM((3,) + half, F32),
        pltpu.VMEM((3,) + half, F32),
        pltpu.VMEM((NZ,) + half, F32),
        pltpu.SemaphoreType.DMA((Total.COPIES,)),
        pltpu.SemaphoreType.DMA((Total.COPIES,)),
    ]


def piece_start(owner):
    return (owner * (GENOUT // 32)) // 128


FLAT = (GENOUT // 128) * MAXB


def unpack(taken, flat, wide, kernel):
    flat[...] = jnp.zeros_like(flat)
    used = COVER * MAXB
    for owner in range(32):
        first = piece_start(owner) * MAXB
        count = min(used, FLAT - first)
        piece = taken[owner // 8, (owner // 4) % 2, (owner // 2) % 2, owner % 2]
        flat[first : first + count, :] += piece.astype(F32)[:count]
    for pixel in range(PIX):
        for part in range(6):
            first = (pixel * 6 + part) * MAXB
            wide[part, pl.ds(pixel, MAXB, stride=PIX), :] = flat[first : first + MAXB, :]
    for part in range(6):
        kernel[:, part * 128 : (part + 1) * 128] = wide[part].astype(BF)


def pack(d_kernel, bias, pieces, wide, flat):
    for part in range(6):
        wide[part] = d_kernel[:, part * 128 : (part + 1) * 128]
        first = (PIX * 6 + part) * MAXB
        flat[first : first + MAXB, :] = bias[0:MAXB, part * 128 : (part + 1) * 128]
    flat[FLAT:, :] = jnp.zeros((flat.shape[0] - FLAT, 128), F32)
    for pixel in range(PIX):
        for part in range(6):
            first = (pixel * 6 + part) * MAXB
            flat[first : first + MAXB, :] = wide[part, pl.ds(pixel, MAXB, stride=PIX), :]
    for owner in range(32):
        first = piece_start(owner) * MAXB
        pieces[owner // 8, (owner // 4) % 2, (owner // 2) % 2, owner % 2] = flat[
            first : first + PIECE, :
        ].astype(BF)


def norm_rows_back(value, upstream, gain):
    normed, scale = standard(value)
    scaled = upstream * gain
    inside = (
        scaled
        - jnp.mean(scaled, axis=-1, keepdims=True)
        - normed * jnp.mean(scaled * normed, axis=-1, keepdims=True)
    )
    return scale * inside, column_sum(upstream * normed), column_sum(upstream)


def close_kernel(
    d_qkv, first, w_qkv, tokens, d_after, params, pixels, kernel, time_loc, late, b_grad,
    hidden, gen_shift, slope, codes, groups, bands,
    out_grad, in_grad, out_q, out_early, pixel_grad,
    d_tokens, grad_q, pieces, crossed, merged, taken, flat, wide, rows, source, early,
    x_send, x_recv, send_sem, recv_sem, local_sem, q_send, q_recv, *rest,
):
    here = z, y, c, x = spot()
    across = device(z, y, c, 1 - x)
    greet([where for _, where in group_peers(z, y, c, x)] + [across])
    scatter = Scatter(
        grad_q, *rest[10:17], out_q, (q_send, q_recv, local_sem), 0, here
    )
    begin = Total(early, out_early, *rest[0:5], here)
    total = Total(source, in_grad, *rest[5:10], here)
    gain = shift = jnp.zeros((1, D), F32)
    for start, count in BANDS:
        band = slice(start, start + count)
        upstream = nt_dot(d_qkv[band, :], w_qkv[...].reshape(D, 3 * D))
        d_norm, gain_part, shift_part = norm_rows_back(tokens[band, :], upstream, params[0:1, :])
        gain += gain_part
        shift += shift_part
        d_tokens[band, :] = (d_after[band, :] + d_norm).astype(BF)
    patches = d_tokens[0:TOK_DEV, :]
    d_kernel = inner_dot(pixels[...], patches)
    live = bands[groups[lax.axis_index("dp")]]
    band_at = lax.broadcasted_iota(jnp.int32, (16, D), 0)
    sums = column_sum(patches.astype(F32)) / live.astype(F32)
    pack(d_kernel, jnp.where(band_at < live, sums, 0.0), pieces, wide, flat)
    order = (2, 1, 3, 0)
    swaps = {}
    for dz in order:
        to = (z + dz) % NZ
        swaps[dz] = remote(
            pieces.at[to, :, :, 1 - x], crossed.at[to], (x_send, x_recv), dz, across
        )
    swaps[2].start()
    swaps[1].start()
    sends = []

    def merge(dz):
        to = (z + dz) % NZ
        swaps[dz].wait_recv()
        if dz in (2, 1):
            swaps[{2: 3, 1: 0}[dz]].start()
        for at_y in range(2):
            for at_c in range(2):
                merged[to, at_y, at_c] = (
                    pieces[to, at_y, at_c, x].astype(F32) + crossed[to, at_y, at_c].astype(F32)
                ).astype(BF)
        for dy in range(2):
            for dc in range(2):
                at_y, at_c = (y + dy) % 2, (c + dc) % 2
                if dz + dy + dc:
                    copy = remote(
                        merged.at[to, at_y, at_c],
                        taken.at[z, y, c],
                        (send_sem, recv_sem),
                        dz * 4 + dy * 2 + dc,
                        device(to, at_y, at_c, x),
                    )
                    copy.start()
                    sends.append(copy)
                else:
                    taken[z, y, c] = merged[z, y, c]

    def grad_third(third):
        part = slice(third * D, (third + 1) * D)
        grad_q[:, :, :, :, part] = (
            inner_dot(first[...], d_qkv[:, part]).astype(BF).reshape(NZ, 2, 2, -1, D)
        )

    grad_third(0)
    merge(2)
    grad_third(1)
    merge(1)
    grad_third(2)
    scatter.stage_a()
    merge(3)
    merge(0)
    extra = d_tokens[TOK_DEV:LIVE, :].astype(F32)
    stamps = jnp.concatenate([extra[2 * m + 1 : 2 * m + 2] for m in range(SLOTS)], axis=0)
    early[0:1, :] = extra[0:1] + extra[2:3] + extra[4:5] + extra[6:7]
    early[1:9, :] = lax.dot_general(
        time_loc[0],
        stamps,
        (((0,), (0,)), ((), ())),
        precision=lax.Precision.HIGHEST,
        preferred_element_type=F32,
    )
    early[9:16, :] = jnp.zeros((7, D), F32)
    early[16:24, :] = late[...]
    early[16:17, :] = gain
    early[17:18, :] = shift
    early[24:32, :] = b_grad[...]
    begin.begin()
    for start, count in BANDS[:2]:
        band = slice(start, start + count)
        pixel_grad[band, :] = nt_dot(d_tokens[band, :], kernel[...])
    scatter.stage_b()
    begin.turn(0)
    for start, count in BANDS[2:4]:
        band = slice(start, start + count)
        pixel_grad[band, :] = nt_dot(d_tokens[band, :], kernel[...])
    scatter.stage_c()
    begin.turn(1)
    for copy in sends:
        copy.wait_recv()
    for n in range(GROUPS):
        block = taken[n // 4, (n // 2) % 2, n % 2].astype(F32)
        for at in range(COVER):
            rows[at, n * MAXB : (n + 1) * MAXB, :] = block[at * MAXB : (at + 1) * MAXB]
    d_hidden = jnp.zeros((GROUPS * MAXB, GEN), F32)
    for at in range(COVER):
        d_hidden += nn_dot(rows[at].astype(BF), gen_shift[at * 128 : (at + 1) * 128, :])
    d_before = d_hidden * slope[...]
    source[0:GEN, :] = lax.dot_general(
        codes[...],
        d_before,
        (((0,), (0,)), ((), ())),
        precision=lax.Precision.HIGHEST,
        preferred_element_type=F32,
    )
    source[GEN:, :] = jnp.broadcast_to(column_sum(d_before), (source.shape[0] - GEN, GEN))
    total.begin()
    low = hidden[...].astype(BF)
    for at in range(COVER // 2):
        out_grad[at * 128 : (at + 1) * 128, :] = inner_dot(rows[at].astype(BF), low)
    total.turn(0)
    scatter.stage_d()
    for at in range(COVER // 2, COVER):
        out_grad[at * 128 : (at + 1) * 128, :] = inner_dot(rows[at].astype(BF), low)
    total.turn(1)
    total.turn(2)
    begin.turn(2)
    total.close()
    scatter.stage_e()
    begin.close()
    begin.finish()
    total.finish()
    for copy in (*sends, *swaps.values()):
        copy.wait_send()


def closing(operands, scalars):
    vmem = pl.BlockSpec(memory_space=pltpu.VMEM)
    smem = pl.BlockSpec(memory_space=pltpu.SMEM)
    small, early = (GEN + 16, GEN), (32, D)
    held = (NZ, 2, 2, PIECE, 128)
    _, _, _, rows, width = operands[2].shape
    return pl.pallas_call(
        close_kernel,
        in_specs=[vmem] * len(operands) + [smem] * len(scalars),
        out_specs=[vmem] * 5,
        out_shape=[
            jax.ShapeDtypeStruct((COVER * 128, GEN), F32),
            jax.ShapeDtypeStruct(small, F32),
            jax.ShapeDtypeStruct((rows, width // 2), F32),
            jax.ShapeDtypeStruct(early, F32),
            jax.ShapeDtypeStruct((TOK_DEV, MAXB * PIX), F32),
        ],
        scratch_shapes=[
            pltpu.VMEM((LIVE, D), BF),
            pltpu.VMEM(operands[2].shape, BF),
            pltpu.VMEM((NZ, 2, 2, 2, PIECE, 128), BF),
            pltpu.VMEM(held, BF),
            pltpu.VMEM(held, BF),
            pltpu.VMEM(held, BF),
            pltpu.VMEM((FLAT + 64, 128), F32),
            pltpu.VMEM((6, MAXB * PIX, 128), F32),
            pltpu.VMEM((COVER, GROUPS * MAXB, 128), F32),
            pltpu.VMEM(small, F32),
            pltpu.VMEM(early, F32),
            pltpu.SemaphoreType.DMA((4,)),
            pltpu.SemaphoreType.DMA((4,)),
            pltpu.SemaphoreType.DMA((16,)),
            pltpu.SemaphoreType.DMA((16,)),
            pltpu.SemaphoreType.DMA((1,)),
            pltpu.SemaphoreType.DMA((8,)),
            pltpu.SemaphoreType.DMA((8,)),
            *total_scratch(early),
            *total_scratch(small),
            *scatter_scratch(rows, width),
        ],
        compiler_params=pltpu.CompilerParams(
            collective_id=2, has_side_effects=True, vmem_limit_bytes=VMEM_ASK
        ),
    )(*operands, *scalars)


def tile_rows(source, first):
    if first + TILE <= LIVE:
        return source[first : first + TILE, :]
    part = source[first:LIVE, :]
    return jnp.concatenate([part, jnp.zeros((first + TILE - LIVE, 128), part.dtype)], axis=0)


def feed_kernel(
    tokens, mixed, top, w_out, vectors, w_up, w_down,
    layer_out, d_after, d_mixed, out_grad, rows, up_grad, down_grad, b_grad,
    second, second_turned, top_full, after, sum_out, sum_second, active, d_upper, proj,
):
    step = pl.program_id(0)

    @pl.when(step == 0)
    def _():
        for first, count in BANDS:
            band = slice(first, first + count)
            value = tokens[band, :] + (nn_dot(mixed[band, :], w_out[...]) + vectors[2:3, :])
            after[band, :] = value
            normed, _ = standard(value)
            put_rows(
                second, first, count, (normed * vectors[3:4, :] + vectors[4:5, :]).astype(BF)
            )
            put_rows(top_full, first, count, top[band, :])
        second_turned[...] = second[...].T
        sum_out[...] = jnp.zeros_like(sum_out)
        b_grad[...] = jnp.zeros_like(b_grad)
        sum_second[...] = jnp.zeros_like(sum_second)

    total = jnp.zeros((1, CHUNK), F32)
    for first, count in BANDS:
        count = -(-count // 16) * 16
        band = slice(first, first + count)
        upper = nn_dot(second[band, :], w_up[...]) + vectors[pl.ds(6 + step, 1), :]
        made, slope = gelu_parts(upper)
        made = made.astype(BF)
        active[band, :] = made
        back = (nt_dot(top_full[band, :], w_down[...]) * slope).astype(BF)
        d_upper[band, :] = back
        total += column_sum(back.astype(F32))
    b_grad[pl.ds(step, 1), :] = total
    sum_out[...] += nn_dot(active[...], w_down[...])
    sum_second[...] += nt_dot(d_upper[...], w_up[...])
    down_grad[...] = inner_dot(active[...], top_full[...]).astype(BF)
    up_grad[...] = nn_dot(second_turned[...], d_upper[...]).astype(BF)

    @pl.when(step == pl.num_programs(0) - 1)
    def _():
        gain = shift = bias = last = jnp.zeros((1, D), F32)
        for first, count in BANDS:
            band = slice(first, first + count)
            value = after[band, :]
            layer_out[band, :] = (value + sum_out[band, :] + vectors[5:6, :]).astype(BF)
            normed, scale = standard(value)
            upstream = sum_second[band, :]
            gain += column_sum(upstream * normed)
            shift += column_sum(upstream)
            scaled = upstream * vectors[3:4, :]
            inside = (
                scaled
                - jnp.mean(scaled, axis=-1, keepdims=True)
                - normed * jnp.mean(scaled * normed, axis=-1, keepdims=True)
            )
            grad_top = top[band, :].astype(F32)
            last += column_sum(grad_top)
            result = grad_top + scale * inside
            d_after[band, :] = result
            low = result.astype(BF)
            bias += column_sum(low.astype(F32))
            put_rows(proj, first, count, low)
            d_mixed[band, :] = nt_dot(low, w_out[...]).astype(BF)
        out_grad[...] = inner_dot(mixed[...], proj[0:LIVE, :]).astype(BF)
        rows[...] = jnp.concatenate([jnp.zeros((2, D), F32), bias, gain, shift, last, jnp.zeros((2, D), F32)], axis=0)


def feed(tokens, mixed, top, w_out, vectors, w_up, w_down):
    width = w_up.shape[1]

    def whole(*shape):
        return pl.BlockSpec(shape, lambda step: (0, 0))

    across = pl.BlockSpec((D, CHUNK), lambda step: (0, step))
    down = pl.BlockSpec((CHUNK, D), lambda step: (step, 0))
    block = whole(LIVE, D)
    return pl.pallas_call(
        feed_kernel,
        grid=(width // CHUNK,),
        in_specs=[block, block, block, whole(D, D), whole(16, D), across, down],
        out_specs=[block, block, block, whole(D, D), whole(8, D), across, down, whole(8, D)],
        out_shape=[
            jax.ShapeDtypeStruct((LIVE, D), BF),
            jax.ShapeDtypeStruct((LIVE, D), F32),
            jax.ShapeDtypeStruct((LIVE, D), BF),
            jax.ShapeDtypeStruct((D, D), BF),
            jax.ShapeDtypeStruct((8, D), F32),
            jax.ShapeDtypeStruct((D, width), BF),
            jax.ShapeDtypeStruct((width, D), BF),
            jax.ShapeDtypeStruct((8, D), F32),
        ],
        scratch_shapes=[
            pltpu.VMEM((ROWS, D), BF),
            pltpu.VMEM((D, ROWS), BF),
            pltpu.VMEM((ROWS, D), BF),
            pltpu.VMEM((LIVE, D), F32),
            pltpu.VMEM((ROWS, D), F32),
            pltpu.VMEM((ROWS, D), F32),
            pltpu.VMEM((ROWS, CHUNK), BF),
            pltpu.VMEM((ROWS, CHUNK), BF),
            pltpu.VMEM((ROWS, D), BF),
        ],
        compiler_params=pltpu.CompilerParams(vmem_limit_bytes=VMEM_ASK),
    )(tokens, mixed, top, w_out, vectors, w_up, w_down)


def three_parts(exact):
    high = exact.astype(BF)
    left = exact - high.astype(F32)
    middle = left.astype(BF)
    return high, middle, (left - middle.astype(F32)).astype(BF)


def attend_back_kernel(
    kind, q_ref, k_ref, v_ref, d_mixed, mixed, log_sum, go, gu, gd,
    out, out_o, out_u, out_d,
    mask_q, mask_k, keys, values, keys_turned, d_query, d_keys, d_values, send_sem, recv_sem, local_sem, *rest,
):
    pair, part = pl.program_id(0), pl.program_id(1)
    here = spot()
    o, u, d = [
        Scatter(
            whole, *rest[7 * at : 7 * at + 7], result, (send_sem, recv_sem, local_sem), 8 * at, here
        )
        for at, (whole, result) in enumerate(((go, out_o), (gu, out_u), (gd, out_d)))
    ]

    plan = {
        0: (lambda: greet(near(*here)), d.stage_a),
        3: (d.stage_b, u.stage_a),
        7: (d.stage_c, o.stage_a),
        13: (u.stage_b,),
        14: (d.stage_d,),
        17: (u.stage_c,),
        22: (d.stage_e,),
        23: (o.stage_b,),
        24: (u.stage_d,),
        25: (o.stage_c,),
        27: (o.stage_d,),
    }

    def transfers(tile):
        for slot, stages in plan.items():
            if slot % TILES == tile:

                @pl.when(pair == slot // TILES)
                def _():
                    for stage in stages:
                        stage()

    @pl.when((pair == 5) & (part == 2))
    def _():
        u.stage_e()
        o.stage_e()

    lane = lax.broadcasted_iota(jnp.int32, (TILE, 128), 1)
    sub = lax.broadcasted_iota(jnp.int32, (128, TILE), 0)

    def with_parts(exact, rest):
        a, b, c = three_parts(exact)
        return jnp.where(
            lane == SLOTS,
            a,
            jnp.where(lane == SLOTS + 1, b, jnp.where(lane == SLOTS + 2, c, rest)),
        )

    @pl.when(part == 0)
    def _():
        transfers(0)

        @pl.when(pair == 0)
        def _():
            mask_rows(kind[0], mask_q, mask_k)
            keys[:, 128:256] = mask_k[...]
            values[:, 128:256] = mask_k[...]

        keys[:, 0:128] = k_ref[0]
        values[:, 0:128] = v_ref[0]
        keys_turned[...] = keys[:, 0:128].T
        d_keys[...] = jnp.zeros_like(d_keys)
        d_values[...] = jnp.zeros_like(d_values)
        for tile in range(TILES):
            first = tile * TILE
            if tile:
                transfers(tile)
            both = q_ref[0, first : first + TILE, :] * BF(0.125)
            up = tile_rows(d_mixed, first)
            logs = log_sum[0, first : first + TILE, :]
            product = up.astype(F32) * tile_rows(mixed, first).astype(F32)
            marks = mask_q[first : first + TILE, :]
            turned = []
            for head in range(2):
                chosen = (lane < HEAD) == (head == 0)
                query = jnp.where(chosen, both, BF(0))
                upstream = jnp.where(chosen, up, BF(0))
                inside = jnp.sum(jnp.where(chosen, product, 0.0), axis=1, keepdims=True)
                wide_query = jnp.concatenate(
                    [query, with_parts(-logs[:, head * HEAD : head * HEAD + 1], marks)], axis=1
                )
                wide_up = jnp.concatenate(
                    [upstream, with_parts(-inside, jnp.zeros_like(marks))], axis=1
                )
                prob = jnp.exp(nt_dot(keys[...], wide_query))
                d_scores = (prob * nt_dot(values[...], wide_up)).astype(BF)
                d_values[...] += nn_dot(prob.astype(BF), upstream)
                d_keys[...] += nn_dot(d_scores, query)
                turned.append(nn_dot(keys_turned[...], d_scores))
            d_query[first : first + TILE, :] = (
                (jnp.where(sub < HEAD, *turned) * 0.125).T.astype(BF)
            )
        out[...] = d_query[0:LIVE, :]

    @pl.when(part == 1)
    def _():
        out[...] = d_keys[0:LIVE, :].astype(BF)

    @pl.when(part == 2)
    def _():
        out[...] = d_values[0:LIVE, :].astype(BF)


def attend_back(kind, qkv, d_mixed, mixed, log_sum, grads):
    def band(first):
        return pl.BlockSpec((LIVE, 128), lambda pair, part: (0, first + pair))

    def head(first):
        return pl.BlockSpec((1, ROWS, 128), lambda pair, part: (first + pair, 0, 0))

    shapes = [grad.shape[3:] for grad in grads]
    outs = [(rows, width // 2) for rows, width in shapes]
    return pl.pallas_call(
        attend_back_kernel,
        grid=(HEADS // 2, 3),
        in_specs=[
            pl.BlockSpec(memory_space=pltpu.SMEM),
            head(0), head(6), head(12), band(0), band(0), head(0),
        ]
        + [pl.BlockSpec(memory_space=pl.ANY)] * 3,
        out_specs=[pl.BlockSpec((LIVE, 128), lambda pair, part: (0, part * 6 + pair))]
        + [pl.BlockSpec(shape, lambda pair, part: (0, 0)) for shape in outs],
        out_shape=[
            jax.ShapeDtypeStruct((LIVE, 3 * D), BF),
            *[jax.ShapeDtypeStruct(shape, F32) for shape in outs],
        ],
        scratch_shapes=[
            pltpu.VMEM((ROWS, 128), BF),
            pltpu.VMEM((ROWS, 128), BF),
            pltpu.VMEM((ROWS, 256), BF),
            pltpu.VMEM((ROWS, 256), BF),
            pltpu.VMEM((128, ROWS), BF),
            pltpu.VMEM((ROWS, 128), BF),
            pltpu.VMEM((ROWS, 128), F32),
            pltpu.VMEM((ROWS, 128), F32),
            pltpu.SemaphoreType.DMA((24,)),
            pltpu.SemaphoreType.DMA((24,)),
            pltpu.SemaphoreType.DMA((3,)),
            *[entry for shape in shapes for entry in scatter_scratch(*shape)],
        ],
        compiler_params=pltpu.CompilerParams(
            collective_id=3, has_side_effects=True, vmem_limit_bytes=VMEM_ASK
        ),
    )(kind, qkv, qkv, qkv, d_mixed, mixed, log_sum, *grads)


def body_block(
    pixels,
    wave_table,
    band_count,
    wave_index,
    group_sensor,
    chip_kind,
    chip_gsd,
    time_loc,
    gen_in,
    gen_bias,
    gen_out,
    meta_weight,
    w_qkv,
    w_out,
    w_up,
    w_down,
    vectors,
    b_up,
    cotangent,
):
    group = lax.axis_index("dp")
    owner = group * 2 + lax.axis_index("fsdp")
    rows, up_rows = vectors.shape[0], b_up.shape[0]

    def steps(count, last):
        falling = 10000.0 ** -(np.arange(count) / last)
        return jnp.asarray(np.tile(np.concatenate([falling, falling]), (8, 1)), F32)

    gen_turned = gen_out.T
    (
        full_q, full_o, full_u, full_d, params, kernel, tokens_in, first, qkv, mixed, log_sum,
        gen_shift, hidden, slope, codes,
    ) = forward(
        (w_qkv, w_out, w_up, w_down),
        (
            pixels,
            vectors.T,
            b_up.reshape(1, -1),
            meta_weight,
            time_loc,
            gen_in,
            gen_bias.reshape(1, -1),
            gen_turned,
            steps(GEN // 2, GEN // 2),
            steps(D // 4, D // 4 - 1),
        ),
        (group_sensor, band_count, wave_index, wave_table, chip_kind, chip_gsd),
    )
    layer_out, d_after, d_mixed, w_out_grad, late, w_up_grad, w_down_grad, b_grad = feed(
        tokens_in,
        mixed,
        cotangent,
        full_o.reshape(D, D),
        params,
        full_u.reshape(D, -1),
        full_d.reshape(-1, D),
    )
    d_qkv, w_out_out, w_up_out, w_down_out = attend_back(
        chip_kind,
        qkv,
        d_mixed,
        mixed,
        log_sum,
        [
            grad.reshape(NZ, 2, 2, -1, grad.shape[1])
            for grad in (w_out_grad, w_up_grad, w_down_grad)
        ],
    )
    gen_out_wide, gen_small, w_qkv_out, summed, pixel_grad = closing(
        (
            d_qkv,
            first,
            full_q,
            tokens_in,
            d_after,
            params,
            pixels,
            kernel,
            time_loc,
            late,
            b_grad,
            hidden,
            gen_shift,
            slope,
            codes,
        ),
        (group_sensor, band_count),
    )
    width = gen_turned.shape[0]
    gen_out_grad = lax.dynamic_slice(
        gen_out_wide, ((owner * width) % 128, 0), (width, GEN)
    ).T
    vectors_out = lax.dynamic_slice(summed, (16, group * rows), (6, rows)).T
    b_up_out = lax.dynamic_slice(
        summed,
        (24 + group // (D // up_rows), (group % (D // up_rows)) * up_rows),
        (1, up_rows),
    ).reshape(-1)
    return (
        layer_out,
        pixel_grad,
        gen_small[:GEN],
        gen_small[GEN],
        gen_out_grad,
        summed[:9],
        w_qkv_out,
        w_out_out,
        w_up_out,
        w_down_out,
        vectors_out,
        b_up_out,
    )


def solution(mesh):
    fits = dict(mesh.shape) == {"dp": 16, "fsdp": 2}
    body = body_block if fits else body_general
    placed = (
        P(("dp", "fsdp"), None),
        P(),
        P(),
        P(),
        P(),
        P(("dp", "fsdp")),
        P(("dp", "fsdp"), None),
        P(("dp", "fsdp"), None, None),
        P(),
        P(),
        P(None, ("dp", "fsdp")),
        P(),
        P("dp", "fsdp"),
        P("dp", "fsdp"),
        P("dp", "fsdp"),
        P("dp", "fsdp"),
        P("dp", None),
        P("dp"),
        P(("dp", "fsdp"), None),
    )
    return jax.shard_map(
        body,
        mesh=mesh,
        in_specs=placed,
        out_specs=(
            P(("dp", "fsdp"), None),
            P(("dp", "fsdp"), None),
            P(),
            P(),
            P(None, ("dp", "fsdp")),
            P(),
            P("dp", "fsdp"),
            P("dp", "fsdp"),
            P("dp", "fsdp"),
            P("dp", "fsdp"),
            P("dp", None),
            P("dp"),
        ),
        check_vma=False,
    )
```

profile of v0, /device:TPU:0, one launch (start us, length us, event | category | flops | bytes accessed | tf_op | source)
XLA Modules:
  0.0 348.8 jit_solution(581263456537271828)
XLA Ops:
  1.3 1.2 reshape.51.b_up
  2.5 128.2 %shard_map.292 = (bf16[4,2,2,48,2304]{4,3,2,1,0:T(8,128)(2,1)}, bf16[4,2,2,48,768]{4,3,2,1,0:T(8,128)(2,1)}, bf16[4,2,2,48,3072]{4,3,2,1,0:T(8,128)(2,1)}, bf16[...) custom-call(bf16[48,1152]{1,0:T(8,128)(2,1)} %wq.1, ...), custom_call_target="tpu_custom_call" | custom-call | tf_op jit(solution)/shard_map/pallas_call | solution.py:845
  130.8 56.0 %shard_map.293 = (bf16[1032,768]{1,0:T(8,128)(2,1)}, f32[1032,768]{1,0:T(8,128)}, bf16[1032,768]{1,0:T(8,128)(2,1)}, bf16[768,768]{1,0:T(8,128)(2,1)}, f32[8,768...) custom-call(f32[1032,768]{1,0:T(8,128)} %get-tuple-element.44.tokens, ...), custom_call_target="tpu_custom_call" | custom-call | tf_op jit(solution)/shard_map/pallas_call | solution.py:1362
  186.7 73.2 %shard_map.294 = (bf16[1032,2304]{1,0:T(8,128)(2,1)}, f32[48,384]{1,0:T(8,128)}, f32[48,1536]{1,0:T(8,128)}, f32[192,384]{1,0:T(8,128)}) custom-call(s32[1]{0:T(128)S(6)} %copy.38.kind, bf16[18,1040,128]{2,1,0:T(8,128)(2,1)} %get-tuple-element.51.q_ref.k_ref.v_ref, bf16[18,1040,128]{2,1,0:T(8,128)(2,1)} %get-tuple-element.51.q_ref.k_ref.v_ref, ...), custom_call_target="tpu_custom_call" | custom-call | tf_op jit(solution)/shard_map/pallas_call | solution.py:1516
  260.0 73.4 %shard_map.295 = (f32[1792,128]{1,0:T(8,128)}, f32[144,128]{1,0:T(8,128)}, f32[48,1152]{1,0:T(8,128)}, f32[32,768]{1,0:T(8,128)}, f32[1024,640]{1,0:T(8,128)}) custom-call(bf16[1032,2304]{1,0:T(8,128)(2,1)} %get-tuple-element.57.d_qkv, bf16[1032,768]{1,0:T(8,128)(2,1)} %get-tuple-element.58.first, bf16[4,2,2,48,2304]{4,3,2,1,0:T(8,128)(2,1)} %get-tuple-element.59.w_qkv, ...), custom_call_target="tpu_custom_call" | custom-call | tf_op jit(solution)/shard_map/pallas_call | solution.py:1237
  333.5 2.1 dynamic-slice_bitcast_fusion
  335.5 0.0 copy-start.2
  335.5 0.0 copy-start.3
  335.5 0.0 copy-start.1
  335.5 1.4 dynamic_slice.11
  337.0 1.5 slice.9
  338.4 1.4 slice.11
  339.8 1.4 dynamic-slice_bitcast_fusion.1
  341.2 1.2 slice_bitcast_fusion
  342.4 0.0 copy-start
  342.4 3.4 copy.39
  345.8 0.0 copy-done.2
  345.8 0.7 copy.40
  346.5 0.0 copy-done.3
  346.5 0.6 copy.41
  347.2 0.0 copy-done.1
  347.2 0.7 copy.42
  347.9 0.0 copy-done
  347.9 0.7 copy.43
Async XLA Ops:
  335.5 10.3 %copy-start.2 = (f32[48,1152]{1,0:T(8,128)S(1)}, f32[48,1152]{1,0:T(8,128)}, u32[]{:S(2)}) copy-start(f32[48,1152]{1,0:T(8,128)} %get-tuple-element.94) | copy-start | bytes 663556
  335.5 11.0 %copy-start.3 = (f32[48,384]{1,0:T(8,128)S(1)}, f32[48,384]{1,0:T(8,128)}, u32[]{:S(2)}) copy-start(f32[48,384]{1,0:T(8,128)} %get-tuple-element.95) | copy-start | bytes 221188
  335.5 11.6 %copy-start.1 = (f32[48,1536]{1,0:T(8,128)S(1)}, f32[48,1536]{1,0:T(8,128)}, u32[]{:S(2)}) copy-start(f32[48,1536]{1,0:T(8,128)} %get-tuple-element.96) | copy-start | bytes 884740
  342.4 5.5 %copy-start = (f32[192,384]{1,0:T(8,128)S(1)}, f32[192,384]{1,0:T(8,128)}, u32[]{:S(2)}) copy-start(f32[192,384]{1,0:T(8,128)} %get-tuple-element.97) | copy-start | bytes 884740
where the time goes:
time: 349 us
  Pallas kernels  331 us (95%)
  local copies, waits for them, and re-layouts  16.4 us (5%)
    pallas_call x1, Pallas kernels, forward(): pl.pallas_call(forward_kernel, out_shape=outs, in_specs=[anywhere] * 4 +...  128 us
    pallas_call x1, Pallas kernels, closing(): pl.pallas_call(close_kernel, in_specs=[vmem] * len(operands) + [smem] * l...  73.4 us
    pallas_call x1, Pallas kernels, attend_back(): pl.pallas_call(attend_back_kernel, grid=(HEADS // 2, 3), in_specs=[pl.Blo...  73.2 us
    pallas_call x1, Pallas kernels, feed(): pl.pallas_call(feed_kernel, grid=(width // CHUNK,), in_specs=[block, bloc...  56 us

commit v1 on v0

--- a/solution.py
+++ b/solution.py
@@ -661,10 +661,17 @@
     peers = group_peers(z, y, c, x)
     across = device(z, y, c, 1 - x)
     greet([where for _, where in peers] + [across])
-    gathers = q, o, u, d = [
+    half = wd.shape[0] // 2
+    gathers = q, o, u, d, e = [
         Gather(shard, whole, (w_send, w_recv), local_sem.at[step], Gather.COPIES * step, lean, here)
         for step, (shard, whole, lean) in enumerate(
-            ((wq, full_q, 3), (wo, full_o, 2), (wu, full_u, 3), (wd, full_d, 2))
+            (
+                (wq, full_q, 4),
+                (wo, full_o, 2),
+                (wu, full_u, 2),
+                (wd.at[0:half], full_d.at[:, :, :, 0:half], 2),
+                (wd.at[half : 2 * half], full_d.at[:, :, :, half : 2 * half], 2),
+            )
         )
     ]
     s_sems = (s_send, s_recv)
@@ -682,7 +689,7 @@
     values[:, 128:256] = jnp.ones((ROWS, 128), BF)
     q.pass_on()
     own_made = pltpu.make_async_copy(
-        made.at[z, y, c], taken.at[z, y, c, x], local_sem.at[4]
+        made.at[z, y, c], taken.at[z, y, c, x], local_sem.at[5]
     )
     own_made.start()
     sends = {}
@@ -696,7 +703,7 @@
         )
         copy.start()
         sends[dz, dy, dc] = copy
-    own_small = pltpu.make_async_copy(small, full_small.at[z, y, c], local_sem.at[5])
+    own_small = pltpu.make_async_copy(small, full_small.at[z, y, c], local_sem.at[6])
     own_small.start()
     small_z = [
         remote(small, full_small.at[z, y, c], s_sems, k - 1, device((z + k) % NZ, y, c, x))
@@ -730,6 +737,9 @@
     part = full_small.at[:, :, c]
     small_c = remote(part, part, s_sems, 4, device(z, y, 1 - c, x))
     small_c.start()
+    u.pass_on()
+    d.send_z()
+    e.send_z()
     unpack(taken, flat, wide, kernel)
     bias = jnp.concatenate(
         [
@@ -752,8 +762,6 @@
             hot = (lane % 64 == spots) & (lane < 192)
             spread.append(nn_dot(jnp.where(hot, 1.0, 0.0).astype(BF), table[...]))
         tokens[band, :] = made_rows + bias + jnp.concatenate(spread, axis=1)
-    u.pass_on()
-    d.send_z()
     small_c.wait_recv()
     params[...] = jnp.zeros_like(params)
     for n in range(GROUPS):
@@ -785,20 +793,25 @@
                 )
 
     def one_pair(pair, carry):
+        @pl.when(pair == 0)
+        def _():
+            u.turn_corner()
+
         @pl.when(pair == 1)
         def _():
             d.pass_on()
+            e.pass_on()
             o.send_z()
-            u.turn_corner()
 
         @pl.when(pair == 2)
         def _():
+            u.share()
             o.pass_on()
 
         @pl.when(pair == 3)
         def _():
             d.turn_corner()
-            u.share()
+            e.turn_corner()
 
         @pl.when(pair == 4)
         def _():
@@ -807,13 +820,14 @@
 
         @pl.when(pair == 5)
         def _():
+            e.share()
             o.share()
 
         attend_pair(pair, qkv, mask_q, mask_k, keys, values, mixed, log_sum)
         return carry
 
     lax.fori_loop(0, HEADS // 2, one_pair, 0)
-    for gather in (o, u, d):
+    for gather in (o, u, d, e):
         gather.receive()
     for gather in gathers:
         gather.finish()
@@ -865,7 +879,7 @@
             pltpu.VMEM((ROWS, 128), BF),
             pltpu.VMEM((ROWS, 128), BF),
         ]
-        + [pltpu.SemaphoreType.DMA((count,)) for count in (76, 76, 6, 5, 5, 20, 20)],
+        + [pltpu.SemaphoreType.DMA((count,)) for count in (95, 95, 7, 5, 5, 20, 20)],
         compiler_params=pltpu.CompilerParams(
             collective_id=0, has_side_effects=True, vmem_limit_bytes=VMEM_ASK
         ),
@@ -903,9 +917,7 @@
         self.core.wait_recv()
         for at_z in range(NZ):
             for at_y in range(2):
-                self.own[at_z, at_y] = (
-                    self.own[at_z, at_y].astype(F32) + self.came[at_z, at_y].astype(F32)
-                ).astype(BF)
+                self.own[at_z, at_y] = self.own[at_z, at_y] + self.came[at_z, at_y]
         self.far_y.start()
         self.far_x.start()
 
@@ -913,15 +925,13 @@
         _, y, _, _ = self.here
         self.far_y.wait_recv()
         for k in range(2):
-            self.own[k, y, :, self.other] = (
-                self.own[k, y, :, self.other].astype(F32) + self.low[k].astype(F32)
-            ).astype(BF)
+            self.own[k, y, :, self.other] = self.own[k, y, :, self.other] + self.low[k]
         self.to_x.start()
         self.far_x.wait_recv()
         for k in range(2):
             self.own[2 + k, 1 - y, :, self.mine] = (
-                self.own[2 + k, 1 - y, :, self.mine].astype(F32) + self.high[k].astype(F32)
-            ).astype(BF)
+                self.own[2 + k, 1 - y, :, self.mine] + self.high[k]
+            )
         self.to_y.start()
 
     def stage_d(self):
@@ -1085,20 +1095,19 @@
 
 
 def close_kernel(
-    d_qkv, first, w_qkv, tokens, d_after, params, pixels, kernel, time_loc, late, b_grad,
+    d_qkv, first, w_qkv, tokens, d_after, params, pixels, kernel, time_loc, late,
     hidden, gen_shift, slope, codes, groups, bands,
-    out_grad, in_grad, out_q, out_early, pixel_grad,
-    d_tokens, grad_q, pieces, crossed, merged, taken, flat, wide, rows, source, early,
+    out_gen, in_grad, in_bias, out_q, out_meta, out_vectors, out_up, pixel_grad,
+    d_tokens, grad_q, pieces, crossed, merged, taken, flat, wide, rows, source, summed, out_grad,
     x_send, x_recv, send_sem, recv_sem, local_sem, q_send, q_recv, *rest,
 ):
     here = z, y, c, x = spot()
     across = device(z, y, c, 1 - x)
     greet([where for _, where in group_peers(z, y, c, x)] + [across])
     scatter = Scatter(
-        grad_q, *rest[10:17], out_q, (q_send, q_recv, local_sem), 0, here
-    )
-    begin = Total(early, out_early, *rest[0:5], here)
-    total = Total(source, in_grad, *rest[5:10], here)
+        grad_q, *rest[5:12], out_q, (q_send, q_recv, local_sem), 0, here
+    )
+    total = Total(source, summed, *rest[0:5], here)
     gain = shift = jnp.zeros((1, D), F32)
     for start, count in BANDS:
         band = slice(start, start + count)
@@ -1166,30 +1175,35 @@
     merge(0)
     extra = d_tokens[TOK_DEV:LIVE, :].astype(F32)
     stamps = jnp.concatenate([extra[2 * m + 1 : 2 * m + 2] for m in range(SLOTS)], axis=0)
-    early[0:1, :] = extra[0:1] + extra[2:3] + extra[4:5] + extra[6:7]
-    early[1:9, :] = lax.dot_general(
-        time_loc[0],
-        stamps,
-        (((0,), (0,)), ((), ())),
-        precision=lax.Precision.HIGHEST,
-        preferred_element_type=F32,
-    )
-    early[9:16, :] = jnp.zeros((7, D), F32)
-    early[16:24, :] = late[...]
-    early[16:17, :] = gain
-    early[17:18, :] = shift
-    early[24:32, :] = b_grad[...]
-    begin.begin()
+    first_rows = jnp.concatenate(
+        [
+            extra[0:1] + extra[2:3] + extra[4:5] + extra[6:7],
+            lax.dot_general(
+                time_loc[0],
+                stamps,
+                (((0,), (0,)), ((), ())),
+                precision=lax.Precision.HIGHEST,
+                preferred_element_type=F32,
+            ),
+            gain,
+            shift,
+            jnp.zeros((5, D), F32),
+        ],
+        axis=0,
+    )
+    meta_at = GEN + 16
+    for part in range(6):
+        source[meta_at + part * 16 : meta_at + part * 16 + 16, :] = first_rows[
+            :, part * 128 : (part + 1) * 128
+        ]
     for start, count in BANDS[:2]:
         band = slice(start, start + count)
         pixel_grad[band, :] = nt_dot(d_tokens[band, :], kernel[...])
     scatter.stage_b()
-    begin.turn(0)
     for start, count in BANDS[2:4]:
         band = slice(start, start + count)
         pixel_grad[band, :] = nt_dot(d_tokens[band, :], kernel[...])
     scatter.stage_c()
-    begin.turn(1)
     for copy in sends:
         copy.wait_recv()
     for n in range(GROUPS):
@@ -1207,7 +1221,7 @@
         precision=lax.Precision.HIGHEST,
         preferred_element_type=F32,
     )
-    source[GEN:, :] = jnp.broadcast_to(column_sum(d_before), (source.shape[0] - GEN, GEN))
+    source[GEN:meta_at, :] = jnp.broadcast_to(column_sum(d_before), (16, GEN))
     total.begin()
     low = hidden[...].astype(BF)
     for at in range(COVER // 2):
@@ -1218,31 +1232,52 @@
         out_grad[at * 128 : (at + 1) * 128, :] = inner_dot(rows[at].astype(BF), low)
     total.turn(1)
     total.turn(2)
-    begin.turn(2)
+    width = out_gen.shape[0]
+    group = lax.axis_index("dp")
+    owner = group * 2 + x
+    out_gen[...] = out_grad[pl.ds(pl.multiple_of((owner * width) % 128, 8), width), :]
     total.close()
     scatter.stage_e()
-    begin.close()
-    begin.finish()
     total.finish()
+    in_grad[...] = summed[0:GEN, :]
+    in_bias[...] = summed[GEN : GEN + 1, :]
+    all_rows = jnp.concatenate(
+        [summed[meta_at + part * 16 : meta_at + part * 16 + 16, :] for part in range(6)], axis=1
+    )
+    out_meta[...] = all_rows[0:9]
+    row = lax.broadcasted_iota(jnp.int32, (8, D), 0)
+    count, up_count = out_vectors.shape[1], out_up.shape[1]
+    per_row = D // up_count
+    norms = jnp.where(
+        row == 0, all_rows[9:10], jnp.where(row == 1, all_rows[10:11], late[0:8, :])
+    )
+    norms = pltpu.roll(norms, (GROUPS - group) % GROUPS * count, 1)
+    out_vectors[...] = norms[0:6, 0:count]
+    ups = pltpu.roll(late[8:16, :], (per_row - group % per_row) % per_row * up_count, 1)
+    out_up[...] = column_sum(jnp.where(row == group // per_row, ups, 0.0))[:, 0:up_count]
     for copy in (*sends, *swaps.values()):
         copy.wait_send()
 
 
-def closing(operands, scalars):
+def closing(operands, scalars, sizes):
     vmem = pl.BlockSpec(memory_space=pltpu.VMEM)
     smem = pl.BlockSpec(memory_space=pltpu.SMEM)
-    small, early = (GEN + 16, GEN), (32, D)
+    small = (GEN + 16 + 96, GEN)
+    width_gen, rows_in, up_rows = sizes
     held = (NZ, 2, 2, PIECE, 128)
     _, _, _, rows, width = operands[2].shape
     return pl.pallas_call(
         close_kernel,
         in_specs=[vmem] * len(operands) + [smem] * len(scalars),
-        out_specs=[vmem] * 5,
+        out_specs=[vmem] * 8,
         out_shape=[
-            jax.ShapeDtypeStruct((COVER * 128, GEN), F32),
-            jax.ShapeDtypeStruct(small, F32),
+            jax.ShapeDtypeStruct((width_gen, GEN), F32),
+            jax.ShapeDtypeStruct((GEN, GEN), F32),
+            jax.ShapeDtypeStruct((1, GEN), F32),
             jax.ShapeDtypeStruct((rows, width // 2), F32),
-            jax.ShapeDtypeStruct(early, F32),
+            jax.ShapeDtypeStruct((9, D), F32),
+            jax.ShapeDtypeStruct((6, rows_in), F32),
+            jax.ShapeDtypeStruct((1, up_rows), F32),
             jax.ShapeDtypeStruct((TOK_DEV, MAXB * PIX), F32),
         ],
         scratch_shapes=[
@@ -1256,7 +1291,8 @@
             pltpu.VMEM((6, MAXB * PIX, 128), F32),
             pltpu.VMEM((COVER, GROUPS * MAXB, 128), F32),
             pltpu.VMEM(small, F32),
-            pltpu.VMEM(early, F32),
+            pltpu.VMEM(small, F32),
+            pltpu.VMEM((COVER * 128, GEN), F32),
             pltpu.SemaphoreType.DMA((4,)),
             pltpu.SemaphoreType.DMA((4,)),
             pltpu.SemaphoreType.DMA((16,)),
@@ -1264,7 +1300,6 @@
             pltpu.SemaphoreType.DMA((1,)),
             pltpu.SemaphoreType.DMA((8,)),
             pltpu.SemaphoreType.DMA((8,)),
-            *total_scratch(early),
             *total_scratch(small),
             *scatter_scratch(rows, width),
         ],
@@ -1397,46 +1432,59 @@
 
 
 def attend_back_kernel(
-    kind, q_ref, k_ref, v_ref, d_mixed, mixed, log_sum, go, gu, gd,
-    out, out_o, out_u, out_d,
+    kind, q_ref, k_ref, v_ref, d_mixed, mixed, log_sum, late, b_grad, go, gu, gd,
+    out, out_o, out_u, out_d, out_late,
     mask_q, mask_k, keys, values, keys_turned, d_query, d_keys, d_values, send_sem, recv_sem, local_sem, *rest,
 ):
     pair, part = pl.program_id(0), pl.program_id(1)
     here = spot()
-    o, u, d = [
+    half = out_d.shape[0] // 2
+    wholes = (go, gu, gd.at[:, :, :, 0:half], gd.at[:, :, :, half : 2 * half])
+    results = (out_o, out_u, out_d.at[0:half], out_d.at[half : 2 * half])
+    o, u, d, e = [
         Scatter(
             whole, *rest[7 * at : 7 * at + 7], result, (send_sem, recv_sem, local_sem), 8 * at, here
         )
-        for at, (whole, result) in enumerate(((go, out_o), (gu, out_u), (gd, out_d)))
+        for at, (whole, result) in enumerate(zip(wholes, results))
     ]
+    late_rows, late_sum, *late_rest = rest[28:]
+    total = Total(late_rows, late_sum, *late_rest, here)
+
+    def begin_total():
+        late_rows[0:8, :] = late[...]
+        late_rows[8:16, :] = b_grad[...]
+        total.begin()
 
     plan = {
-        0: (lambda: greet(near(*here)), d.stage_a),
-        3: (d.stage_b, u.stage_a),
-        7: (d.stage_c, o.stage_a),
-        13: (u.stage_b,),
-        14: (d.stage_d,),
-        17: (u.stage_c,),
-        22: (d.stage_e,),
-        23: (o.stage_b,),
-        24: (u.stage_d,),
-        25: (o.stage_c,),
-        27: (o.stage_d,),
+        0: (lambda: greet(near(*here)), u.stage_a),
+        1: (u.stage_b, d.stage_a),
+        2: (e.stage_a, o.stage_a, begin_total),
+        3: (u.stage_c,),
+        4: (lambda: total.turn(0),),
+        5: (d.stage_b,),
+        6: (d.stage_c, u.stage_d, e.stage_b),
+        7: (e.stage_c, lambda: total.turn(1)),
+        8: (d.stage_d, o.stage_b),
+        9: (e.stage_d, u.stage_e, o.stage_c, lambda: total.turn(2)),
+        10: (o.stage_d, d.stage_e),
+        11: (total.close,),
     }
 
-    def transfers(tile):
+    def transfers(half):
         for slot, stages in plan.items():
-            if slot % TILES == tile:
-
-                @pl.when(pair == slot // TILES)
+            if slot % 2 == half:
+
+                @pl.when(pair == slot // 2)
                 def _():
                     for stage in stages:
                         stage()
 
     @pl.when((pair == 5) & (part == 2))
     def _():
-        u.stage_e()
+        e.stage_e()
         o.stage_e()
+        total.finish()
+        out_late[...] = late_sum[...]
 
     lane = lax.broadcasted_iota(jnp.int32, (TILE, 128), 1)
     sub = lax.broadcasted_iota(jnp.int32, (128, TILE), 0)
@@ -1466,8 +1514,8 @@
         d_values[...] = jnp.zeros_like(d_values)
         for tile in range(TILES):
             first = tile * TILE
-            if tile:
-                transfers(tile)
+            if tile == 3:
+                transfers(1)
             both = q_ref[0, first : first + TILE, :] * BF(0.125)
             up = tile_rows(d_mixed, first)
             logs = log_sum[0, first : first + TILE, :]
@@ -1504,28 +1552,35 @@
         out[...] = d_values[0:LIVE, :].astype(BF)
 
 
-def attend_back(kind, qkv, d_mixed, mixed, log_sum, grads):
+def attend_back(kind, qkv, d_mixed, mixed, log_sum, late, b_grad, grads):
     def band(first):
         return pl.BlockSpec((LIVE, 128), lambda pair, part: (0, first + pair))
 
+    def row_block(count):
+        return pl.BlockSpec((count, D), lambda pair, part: (0, 0))
+
     def head(first):
         return pl.BlockSpec((1, ROWS, 128), lambda pair, part: (first + pair, 0, 0))
 
     shapes = [grad.shape[3:] for grad in grads]
     outs = [(rows, width // 2) for rows, width in shapes]
+    low = (shapes[2][0] // 2, shapes[2][1])
+    parts = [*shapes[:2], low, low]
     return pl.pallas_call(
         attend_back_kernel,
         grid=(HEADS // 2, 3),
         in_specs=[
             pl.BlockSpec(memory_space=pltpu.SMEM),
-            head(0), head(6), head(12), band(0), band(0), head(0),
+            head(0), head(6), head(12), band(0), band(0), head(0), row_block(8), row_block(8),
         ]
         + [pl.BlockSpec(memory_space=pl.ANY)] * 3,
         out_specs=[pl.BlockSpec((LIVE, 128), lambda pair, part: (0, part * 6 + pair))]
-        + [pl.BlockSpec(shape, lambda pair, part: (0, 0)) for shape in outs],
+        + [pl.BlockSpec(shape, lambda pair, part: (0, 0)) for shape in outs]
+        + [row_block(16)],
         out_shape=[
             jax.ShapeDtypeStruct((LIVE, 3 * D), BF),
             *[jax.ShapeDtypeStruct(shape, F32) for shape in outs],
+            jax.ShapeDtypeStruct((16, D), F32),
         ],
         scratch_shapes=[
             pltpu.VMEM((ROWS, 128), BF),
@@ -1536,15 +1591,18 @@
             pltpu.VMEM((ROWS, 128), BF),
             pltpu.VMEM((ROWS, 128), F32),
             pltpu.VMEM((ROWS, 128), F32),
-            pltpu.SemaphoreType.DMA((24,)),
-            pltpu.SemaphoreType.DMA((24,)),
-            pltpu.SemaphoreType.DMA((3,)),
-            *[entry for shape in shapes for entry in scatter_scratch(*shape)],
+            pltpu.SemaphoreType.DMA((32,)),
+            pltpu.SemaphoreType.DMA((32,)),
+            pltpu.SemaphoreType.DMA((4,)),
+            *[entry for shape in parts for entry in scatter_scratch(*shape)],
+            pltpu.VMEM((16, D), F32),
+            pltpu.VMEM((16, D), F32),
+            *total_scratch((16, D)),
         ],
         compiler_params=pltpu.CompilerParams(
             collective_id=3, has_side_effects=True, vmem_limit_bytes=VMEM_ASK
         ),
-    )(kind, qkv, qkv, qkv, d_mixed, mixed, log_sum, *grads)
+    )(kind, qkv, qkv, qkv, d_mixed, mixed, log_sum, late, b_grad, *grads)
 
 
 def body_block(
@@ -1568,8 +1626,6 @@
     b_up,
     cotangent,
 ):
-    group = lax.axis_index("dp")
-    owner = group * 2 + lax.axis_index("fsdp")
     rows, up_rows = vectors.shape[0], b_up.shape[0]
 
     def steps(count, last):
@@ -1605,60 +1661,54 @@
         full_u.reshape(D, -1),
         full_d.reshape(-1, D),
     )
-    d_qkv, w_out_out, w_up_out, w_down_out = attend_back(
+    d_qkv, w_out_out, w_up_out, w_down_out, late_sum = attend_back(
         chip_kind,
         qkv,
         d_mixed,
         mixed,
         log_sum,
+        late,
+        b_grad,
         [
             grad.reshape(NZ, 2, 2, -1, grad.shape[1])
             for grad in (w_out_grad, w_up_grad, w_down_grad)
         ],
     )
-    gen_out_wide, gen_small, w_qkv_out, summed, pixel_grad = closing(
-        (
-            d_qkv,
-            first,
-            full_q,
-            tokens_in,
-            d_after,
-            params,
-            pixels,
-            kernel,
-            time_loc,
-            late,
-            b_grad,
-            hidden,
-            gen_shift,
-            slope,
-            codes,
-        ),
-        (group_sensor, band_count),
-    )
-    width = gen_turned.shape[0]
-    gen_out_grad = lax.dynamic_slice(
-        gen_out_wide, ((owner * width) % 128, 0), (width, GEN)
-    ).T
-    vectors_out = lax.dynamic_slice(summed, (16, group * rows), (6, rows)).T
-    b_up_out = lax.dynamic_slice(
-        summed,
-        (24 + group // (D // up_rows), (group % (D // up_rows)) * up_rows),
-        (1, up_rows),
-    ).reshape(-1)
+    gen_out_grad, gen_in_grad, gen_bias_grad, w_qkv_out, meta_grad, vectors_out, b_up_out, pixel_grad = (
+        closing(
+            (
+                d_qkv,
+                first,
+                full_q,
+                tokens_in,
+                d_after,
+                params,
+                pixels,
+                kernel,
+                time_loc,
+                late_sum,
+                hidden,
+                gen_shift,
+                slope,
+                codes,
+            ),
+            (group_sensor, band_count),
+            (gen_turned.shape[0], rows, up_rows),
+        )
+    )
     return (
         layer_out,
         pixel_grad,
-        gen_small[:GEN],
-        gen_small[GEN],
-        gen_out_grad,
-        summed[:9],
+        gen_in_grad,
+        gen_bias_grad.reshape(-1),
+        gen_out_grad.T,
+        meta_grad,
         w_qkv_out,
         w_out_out,
         w_up_out,
         w_down_out,
-        vectors_out,
-        b_up_out,
+        vectors_out.T,
+        b_up_out.reshape(-1),
     )
 
 

time: 349 us -> 334 us (0.957)
  Pallas kernels: 331 us -> 320 us
  local copies, waits for them, and re-layouts: 16.4 us -> 11.3 us
    pallas_call x1, Pallas kernels: 128 us -> 117 us  [forward(): pl.pallas_call(forward_kernel, out_shape=outs, in_specs=[anywhere] * 4 +...]
    unnamed x13 -> x31, local copies, waits for them, and re-layouts: 6.2 us -> 10.1 us
where the time goes in v1:
time: 334 us; the launch traced here: 333 us
  Pallas kernels  320 us (96%)
  local copies, waits for them, and re-layouts  11.3 us (3%)
    pallas_call x1, Pallas kernels, forward(): pl.pallas_call(forward_kernel, out_shape=outs, in_specs=[anywhere] * 4 +...  117 us
    pallas_call x1, Pallas kernels, attend_back(): pl.pallas_call(attend_back_kernel, grid=(HEADS // 2, 3), in_specs=[pl.Blo...  76.5 us
    pallas_call x1, Pallas kernels, closing(): pl.pallas_call(close_kernel, in_specs=[vmem] * len(operands) + [smem] * l...  71.1 us
    pallas_call x1, Pallas kernels, feed(): pl.pallas_call(feed_kernel, grid=(width // CHUNK,), in_specs=[block, bloc...  56 us
    unnamed x31, local copies, waits for them, and re-layouts  10.1 us

profile of v1, /device:TPU:0, one launch (start us, length us, event | category | flops | bytes accessed | tf_op | source)
XLA Modules:
  0.0 333.2 jit_solution(17544381249475210345)
XLA Ops:
  1.3 1.2 reshape.54.b_up
  2.5 116.7 %shard_map.292 = (bf16[4,2,2,48,2304]{4,3,2,1,0:T(8,128)(2,1)}, bf16[4,2,2,48,768]{4,3,2,1,0:T(8,128)(2,1)}, bf16[4,2,2,48,3072]{4,3,2,1,0:T(8,128)(2,1)}, bf16[...) custom-call(bf16[48,1152]{1,0:T(8,128)(2,1)} %wq.1, ...), custom_call_target="tpu_custom_call" | custom-call | tf_op jit(solution)/shard_map/pallas_call | solution.py:859
  119.2 56.0 %shard_map.293 = (bf16[1032,768]{1,0:T(8,128)(2,1)}, f32[1032,768]{1,0:T(8,128)}, bf16[1032,768]{1,0:T(8,128)(2,1)}, bf16[768,768]{1,0:T(8,128)(2,1)}, f32[8,768...) custom-call(f32[1032,768]{1,0:T(8,128)} %get-tuple-element.48.tokens, ...), custom_call_target="tpu_custom_call" | custom-call | tf_op jit(solution)/shard_map/pallas_call | solution.py:1397
  175.2 76.5 %shard_map.294 = (bf16[1032,2304]{1,0:T(8,128)(2,1)}, f32[48,384]{1,0:T(8,128)}, f32[48,1536]{1,0:T(8,128)}, f32[192,384]{1,0:T(8,128)}, f32[16,768]{1,0:T(8,128)}) custom-call(s32[1]{0:T(128)S(6)} %copy.44.kind, bf16[18,1040,128]{2,1,0:T(8,128)(2,1)} %get-tuple-element.55.q_ref.k_ref.v_ref, bf16[18,1040,128]{2,1,0:T(8,128)(2,1)} %get-tuple-element.55.q_ref.k_ref.v_ref, ...), custom_call_target="tpu_custom_call" | custom-call | tf_op jit(solution)/shard_map/pallas_call | solution.py:1569
  251.7 71.1 %shard_map.295 = (f32[1560,128]{1,0:T(8,128)}, f32[128,128]{1,0:T(8,128)}, f32[1,128]{1,0:T(1,128)}, f32[48,1152]{1,0:T(8,128)}, f32[9,768]{1,0:T(8,128)}, /*ind...) custom-call(bf16[1032,2304]{1,0:T(8,128)(2,1)} %get-tuple-element.63.d_qkv, ...), custom_call_target="tpu_custom_call" | custom-call | tf_op jit(solution)/shard_map/pallas_call | solution.py:1269
  322.8 0.0 copy-start.5
  322.8 0.0 copy-start.9
  322.8 0.0 copy-start
  322.8 0.0 copy-start.6
  322.8 0.0 copy-start.3
  322.8 0.0 copy-start.4
  322.9 3.5 %copy.45 = f32[1024,640]{1,0:T(8,128)} copy(f32[1024,640]{1,0:T(8,128)} %get-tuple-element.97) | data formatting | bytes 5242880
  326.4 0.6 copy.46
  327.0 0.5 copy.47
  327.5 0.9 copy.48
  328.4 0.6 copy.49
  329.1 0.7 copy.50
  329.7 0.6 copy.51
  330.4 0.7 copy.52
  331.1 0.0 copy-done.1
  331.1 0.7 copy.53
  331.8 0.0 copy-done.7
  331.8 0.6 copy.54
  332.4 0.6 copy.55
  (12 shorter events, 0.0 us)
Async XLA Ops:
  322.8 3.6 %copy-start.5 = (f32[128,128]{1,0:T(8,128)S(1)}, f32[128,128]{1,0:T(8,128)}, u32[]{:S(2)}) copy-start(f32[128,128]{1,0:T(8,128)} %get-tuple-element.98) | copy-start | bytes 196612
  322.8 4.2 %copy-start.9 = (f32[1,128]{1,0:T(1,128)S(1)}, f32[1,128]{1,0:T(1,128)}, u32[]{:S(2)}) copy-start(f32[1,128]{1,0:T(1,128)} %get-tuple-element.75) | copy-start | bytes 1540
  322.8 4.7 %copy-start = (f32[1560,128]{1,0:T(8,128)S(1)}, f32[1560,128]{1,0:T(8,128)}, u32[]{:S(2)}) copy-start(f32[1560,128]{1,0:T(8,128)} %get-tuple-element.76) | copy-start | bytes 2396164
  322.8 5.6 %copy-start.6 = (f32[9,768]{1,0:T(8,128)S(1)}, f32[9,768]{1,0:T(8,128)}, u32[]{:S(2)}) copy-start(f32[9,768]{1,0:T(8,128)} %get-tuple-element.101) | copy-start | bytes 82948
  322.8 6.2 %copy-start.3 = (f32[48,1152]{1,0:T(8,128)S(1)}, f32[48,1152]{1,0:T(8,128)}, u32[]{:S(2)}) copy-start(f32[48,1152]{1,0:T(8,128)} %get-tuple-element.102) | copy-start | bytes 663556
  322.8 6.9 %copy-start.4 = (f32[48,384]{1,0:T(8,128)S(1)}, f32[48,384]{1,0:T(8,128)}, u32[]{:S(2)}) copy-start(f32[48,384]{1,0:T(8,128)} %get-tuple-element.103) | copy-start | bytes 221188
  322.8 7.5 %copy-start.2 = (f32[48,1536]{1,0:T(8,128)S(1)}, f32[48,1536]{1,0:T(8,128)}, u32[]{:S(2)}) copy-start(f32[48,1536]{1,0:T(8,128)} %get-tuple-element.104) | copy-start | bytes 884740
  322.9 8.2 %copy-start.1 = (f32[192,384]{1,0:T(8,128)S(1)}, f32[192,384]{1,0:T(8,128)}, u32[]{:S(2)}) copy-start(f32[192,384]{1,0:T(8,128)} %get-tuple-element.105) | copy-start | bytes 884740
  322.9 9.0 %copy-start.7 = (f32[6,48]{1,0:T(8,128)S(1)}, f32[6,48]{1,0:T(8,128)}, u32[]{:S(2)}) copy-start(f32[6,48]{1,0:T(8,128)} %get-tuple-element.82) | copy-start | bytes 3460
  322.9 9.5 %copy-start.8 = (f32[1,192]{1,0:T(1,128)S(1)}, f32[1,192]{1,0:T(1,128)}, u32[]{:S(2)}) copy-start(f32[1,192]{1,0:T(1,128)} %get-tuple-element.83) | copy-start | bytes 2308

commit v2 on v1

--- a/solution.py
+++ b/solution.py
@@ -353,6 +353,7 @@
 ROWS = 1040
 TILE = 208
 TILES = 5
+WIDE = 520
 NZ = 4
 GROUPS = 16
 PIECE = 144
@@ -622,19 +623,19 @@
 
 
 def attend_pair(pair, qkv, mask_q, mask_k, keys, values, mixed, log_sum):
-    lane = lax.broadcasted_iota(jnp.int32, (TILE, 128), 1)
+    lane = lax.broadcasted_iota(jnp.int32, (WIDE, 128), 1)
     lanes = pl.ds(pl.multiple_of(pair * 128, 128), 128)
     keys[:, 0:128] = qkv[6 + pair]
     keys[:, 128:256] = mask_k[...]
     values[:, 0:128] = qkv[12 + pair]
-    for tile in range(TILES):
-        first = tile * TILE
-        both = qkv[pair, first : first + TILE, :] * BF(0.125)
+    for tile in range((ROWS // WIDE)):
+        first = tile * WIDE
+        both = qkv[pair, first : first + WIDE, :] * BF(0.125)
         results, sums = [], []
         for head in range(2):
             query = jnp.where((lane < HEAD) == (head == 0), both, BF(0))
             scores = nt_dot(
-                jnp.concatenate([query, mask_q[first : first + TILE, :]], axis=1), keys[...]
+                jnp.concatenate([query, mask_q[first : first + WIDE, :]], axis=1), keys[...]
             )
             peak = jnp.max(scores, axis=1, keepdims=True)
             expo = jnp.exp(scores - peak).astype(BF)
@@ -642,9 +643,9 @@
             totals = made[:, 128:256]
             results.append(made[:, 0:128] / totals)
             sums.append(peak + jnp.log(totals))
-        count = min(TILE, LIVE - first)
+        count = min(WIDE, LIVE - first)
         mixed[first : first + count, lanes] = jnp.where(lane < HEAD, *results)[:count].astype(BF)
-        log_sum[pair, first : first + TILE, :] = jnp.where(lane < HEAD, *sums)
+        log_sum[pair, first : first + WIDE, :] = jnp.where(lane < HEAD, *sums)
 
 
 def forward_kernel(

time: 334 us -> 331 us (level)
    pallas_call x1, Pallas kernels: 117 us -> 113 us  [forward(): pl.pallas_call(forward_kernel, out_shape=outs, in_specs=[anywhere] * 4 +...]
where the time goes in v2:
time: 331 us; the launch traced here: 330 us
  Pallas kernels  317 us (96%)
  local copies, waits for them, and re-layouts  11.3 us (3%)
    pallas_call x1, Pallas kernels, forward(): pl.pallas_call(forward_kernel, out_shape=outs, in_specs=[anywhere] * 4 +...  113 us
    pallas_call x1, Pallas kernels, attend_back(): pl.pallas_call(attend_back_kernel, grid=(HEADS // 2, 3), in_specs=[pl.Blo...  76.4 us
    pallas_call x1, Pallas kernels, closing(): pl.pallas_call(close_kernel, in_specs=[vmem] * len(operands) + [smem] * l...  71.8 us
    pallas_call x1, Pallas kernels, feed(): pl.pallas_call(feed_kernel, grid=(width // CHUNK,), in_specs=[block, bloc...  56 us
    unnamed x31, local copies, waits for them, and re-layouts  10.1 us

profile of v2, /device:TPU:0, one launch (start us, length us, event | category | flops | bytes accessed | tf_op | source)
XLA Modules:
  0.0 330.4 jit_solution(15311080505693812530)
XLA Ops:
  1.3 1.2 reshape.54.b_up
  2.5 113.3 %shard_map.292 = (bf16[4,2,2,48,2304]{4,3,2,1,0:T(8,128)(2,1)}, bf16[4,2,2,48,768]{4,3,2,1,0:T(8,128)(2,1)}, bf16[4,2,2,48,3072]{4,3,2,1,0:T(8,128)(2,1)}, bf16[...) custom-call(bf16[48,1152]{1,0:T(8,128)(2,1)} %wq.1, ...), custom_call_target="tpu_custom_call" | custom-call | tf_op jit(solution)/shard_map/pallas_call | solution.py:860
  115.8 56.0 %shard_map.293 = (bf16[1032,768]{1,0:T(8,128)(2,1)}, f32[1032,768]{1,0:T(8,128)}, bf16[1032,768]{1,0:T(8,128)(2,1)}, bf16[768,768]{1,0:T(8,128)(2,1)}, f32[8,768...) custom-call(f32[1032,768]{1,0:T(8,128)} %get-tuple-element.48.tokens, ...), custom_call_target="tpu_custom_call" | custom-call | tf_op jit(solution)/shard_map/pallas_call | solution.py:1398
  171.8 76.4 %shard_map.294 = (bf16[1032,2304]{1,0:T(8,128)(2,1)}, f32[48,384]{1,0:T(8,128)}, f32[48,1536]{1,0:T(8,128)}, f32[192,384]{1,0:T(8,128)}, f32[16,768]{1,0:T(8,128)}) custom-call(s32[1]{0:T(128)S(6)} %copy.44.kind, bf16[18,1040,128]{2,1,0:T(8,128)(2,1)} %get-tuple-element.55.q_ref.k_ref.v_ref, bf16[18,1040,128]{2,1,0:T(8,128)(2,1)} %get-tuple-element.55.q_ref.k_ref.v_ref, ...), custom_call_target="tpu_custom_call" | custom-call | tf_op jit(solution)/shard_map/pallas_call | solution.py:1570
  248.2 71.8 %shard_map.295 = (f32[1560,128]{1,0:T(8,128)}, f32[128,128]{1,0:T(8,128)}, f32[1,128]{1,0:T(1,128)}, f32[48,1152]{1,0:T(8,128)}, f32[9,768]{1,0:T(8,128)}, /*ind...) custom-call(bf16[1032,2304]{1,0:T(8,128)(2,1)} %get-tuple-element.63.d_qkv, ...), custom_call_target="tpu_custom_call" | custom-call | tf_op jit(solution)/shard_map/pallas_call | solution.py:1270
  320.0 0.0 copy-start.5
  320.0 0.0 copy-start.9
  320.0 0.0 copy-start
  320.0 0.0 copy-start.6
  320.0 0.0 copy-start.3
  320.0 0.0 copy-start.4
  320.0 0.0 copy-start.2
  320.1 0.0 copy-start.1
  320.1 3.5 %copy.45 = f32[1024,640]{1,0:T(8,128)} copy(f32[1024,640]{1,0:T(8,128)} %get-tuple-element.97) | data formatting | bytes 5242880
  323.6 0.6 copy.46
  324.2 0.5 copy.47
  324.7 0.9 copy.48
  325.6 0.6 copy.49
  326.3 0.7 copy.50
  326.9 0.6 copy.51
  327.6 0.7 copy.52
  328.3 0.7 copy.53
  329.0 0.6 copy.54
  329.6 0.6 copy.55
  (12 shorter events, 0.0 us)
Async XLA Ops:
  320.0 3.6 %copy-start.5 = (f32[128,128]{1,0:T(8,128)S(1)}, f32[128,128]{1,0:T(8,128)}, u32[]{:S(2)}) copy-start(f32[128,128]{1,0:T(8,128)} %get-tuple-element.98) | copy-start | bytes 196612
  320.0 4.2 %copy-start.9 = (f32[1,128]{1,0:T(1,128)S(1)}, f32[1,128]{1,0:T(1,128)}, u32[]{:S(2)}) copy-start(f32[1,128]{1,0:T(1,128)} %get-tuple-element.75) | copy-start | bytes 1540
  320.0 4.7 %copy-start = (f32[1560,128]{1,0:T(8,128)S(1)}, f32[1560,128]{1,0:T(8,128)}, u32[]{:S(2)}) copy-start(f32[1560,128]{1,0:T(8,128)} %get-tuple-element.76) | copy-start | bytes 2396164
  320.0 5.6 %copy-start.6 = (f32[9,768]{1,0:T(8,128)S(1)}, f32[9,768]{1,0:T(8,128)}, u32[]{:S(2)}) copy-start(f32[9,768]{1,0:T(8,128)} %get-tuple-element.101) | copy-start | bytes 82948
  320.0 6.2 %copy-start.3 = (f32[48,1152]{1,0:T(8,128)S(1)}, f32[48,1152]{1,0:T(8,128)}, u32[]{:S(2)}) copy-start(f32[48,1152]{1,0:T(8,128)} %get-tuple-element.102) | copy-start | bytes 663556
  320.0 6.9 %copy-start.4 = (f32[48,384]{1,0:T(8,128)S(1)}, f32[48,384]{1,0:T(8,128)}, u32[]{:S(2)}) copy-start(f32[48,384]{1,0:T(8,128)} %get-tuple-element.103) | copy-start | bytes 221188
  320.0 7.5 %copy-start.2 = (f32[48,1536]{1,0:T(8,128)S(1)}, f32[48,1536]{1,0:T(8,128)}, u32[]{:S(2)}) copy-start(f32[48,1536]{1,0:T(8,128)} %get-tuple-element.104) | copy-start | bytes 884740
  320.1 8.2 %copy-start.1 = (f32[192,384]{1,0:T(8,128)S(1)}, f32[192,384]{1,0:T(8,128)}, u32[]{:S(2)}) copy-start(f32[192,384]{1,0:T(8,128)} %get-tuple-element.105) | copy-start | bytes 884740
  320.1 9.0 %copy-start.7 = (f32[6,48]{1,0:T(8,128)S(1)}, f32[6,48]{1,0:T(8,128)}, u32[]{:S(2)}) copy-start(f32[6,48]{1,0:T(8,128)} %get-tuple-element.82) | copy-start | bytes 3460
  320.1 9.5 %copy-start.8 = (f32[1,192]{1,0:T(1,128)S(1)}, f32[1,192]{1,0:T(1,128)}, u32[]{:S(2)}) copy-start(f32[1,192]{1,0:T(1,128)} %get-tuple-element.83) | copy-start | bytes 2308

commit v3 on v2

--- a/solution.py
+++ b/solution.py
@@ -531,11 +531,11 @@
 
 def make_small(vectors, b_up, held, small):
     group = lax.axis_index("dp")
-    count, up_count = vectors.shape[1], b_up.shape[1]
+    count, up_count = vectors.shape[1], b_up.shape[0]
     per_row = D // up_count
     held[...] = jnp.zeros_like(held)
     held[0:6, 0:count] = vectors[...].astype(F32)
-    held[8:9, 0:up_count] = b_up[...].astype(F32)
+    held[8:9, 0:up_count] = b_up[...].astype(F32).reshape(1, up_count)
     rows = pltpu.roll(held[0:8, :], group * count, 1)
     bias = pltpu.roll(held[8:16, :], (group % per_row) * up_count, 1)[0:1]
     row = lax.broadcasted_iota(jnp.int32, (8, D), 0)
@@ -1320,7 +1320,7 @@
 def feed_kernel(
     tokens, mixed, top, w_out, vectors, w_up, w_down,
     layer_out, d_after, d_mixed, out_grad, rows, up_grad, down_grad, b_grad,
-    second, second_turned, top_full, after, sum_out, sum_second, active, d_upper, proj,
+    second, second_turned, top_full, after, sum_out, sum_second, active, d_upper, proj, wide_up, wide_back,
 ):
     step = pl.program_id(0)
 
@@ -1340,15 +1340,17 @@
         b_grad[...] = jnp.zeros_like(b_grad)
         sum_second[...] = jnp.zeros_like(sum_second)
 
+    wide_up[...] = nn_dot(second[...], w_up[...])
+    wide_back[...] = nt_dot(top_full[...], w_down[...])
     total = jnp.zeros((1, CHUNK), F32)
     for first, count in BANDS:
         count = -(-count // 16) * 16
         band = slice(first, first + count)
-        upper = nn_dot(second[band, :], w_up[...]) + vectors[pl.ds(6 + step, 1), :]
+        upper = wide_up[band, :] + vectors[pl.ds(6 + step, 1), :]
         made, slope = gelu_parts(upper)
         made = made.astype(BF)
         active[band, :] = made
-        back = (nt_dot(top_full[band, :], w_down[...]) * slope).astype(BF)
+        back = (wide_back[band, :] * slope).astype(BF)
         d_upper[band, :] = back
         total += column_sum(back.astype(F32))
     b_grad[pl.ds(step, 1), :] = total
@@ -1390,7 +1392,7 @@
     width = w_up.shape[1]
 
     def whole(*shape):
-        return pl.BlockSpec(shape, lambda step: (0, 0))
+        return pl.BlockSpec(shape, lambda step: (0, 0), pipeline_mode=pl.Buffered(1))
 
     across = pl.BlockSpec((D, CHUNK), lambda step: (0, step))
     down = pl.BlockSpec((CHUNK, D), lambda step: (step, 0))
@@ -1399,7 +1401,7 @@
         feed_kernel,
         grid=(width // CHUNK,),
         in_specs=[block, block, block, whole(D, D), whole(16, D), across, down],
-        out_specs=[block, block, block, whole(D, D), whole(8, D), across, down, whole(8, D)],
+        out_specs=[pl.BlockSpec((LIVE, D), lambda step: (0, 0))] * 3 + [pl.BlockSpec((D, D), lambda step: (0, 0)), pl.BlockSpec((8, D), lambda step: (0, 0)), across, down, pl.BlockSpec((8, D), lambda step: (0, 0))],
         out_shape=[
             jax.ShapeDtypeStruct((LIVE, D), BF),
             jax.ShapeDtypeStruct((LIVE, D), F32),
@@ -1420,6 +1422,8 @@
             pltpu.VMEM((ROWS, CHUNK), BF),
             pltpu.VMEM((ROWS, CHUNK), BF),
             pltpu.VMEM((ROWS, D), BF),
+            pltpu.VMEM((ROWS, CHUNK), F32),
+            pltpu.VMEM((ROWS, CHUNK), F32),
         ],
         compiler_params=pltpu.CompilerParams(vmem_limit_bytes=VMEM_ASK),
     )(tokens, mixed, top, w_out, vectors, w_up, w_down)
@@ -1642,7 +1646,7 @@
         (
             pixels,
             vectors.T,
-            b_up.reshape(1, -1),
+            b_up,
             meta_weight,
             time_loc,
             gen_in,

time: 331 us -> 328 us (level)
  no operation moved by 1% of the time
where the time goes in v3:
time: 328 us
  Pallas kernels  316 us (96%)
  local copies, waits for them, and re-layouts  10.1 us (3%)
    pallas_call x1, Pallas kernels, forward(): pl.pallas_call(forward_kernel, out_shape=outs, in_specs=[anywhere] * 4 +...  113 us
    pallas_call x1, Pallas kernels, attend_back(): pl.pallas_call(attend_back_kernel, grid=(HEADS // 2, 3), in_specs=[pl.Blo...  76.4 us
    pallas_call x1, Pallas kernels, closing(): pl.pallas_call(close_kernel, in_specs=[vmem] * len(operands) + [smem] * l...  71.8 us
    pallas_call x1, Pallas kernels, feed(): pl.pallas_call(feed_kernel, grid=(width // CHUNK,), in_specs=[block, bloc...  55.1 us
    unnamed x31, local copies, waits for them, and re-layouts  10.1 us

profile of v3, /device:TPU:0, one launch (start us, length us, event | category | flops | bytes accessed | tf_op | source)
XLA Modules:
  0.0 327.9 jit_solution(5432121270035880932)
XLA Ops:
  1.3 112.9 %shard_map.292 = (bf16[4,2,2,48,2304]{4,3,2,1,0:T(8,128)(2,1)}, bf16[4,2,2,48,768]{4,3,2,1,0:T(8,128)(2,1)}, bf16[4,2,2,48,3072]{4,3,2,1,0:T(8,128)(2,1)}, bf16[...) custom-call(bf16[48,1152]{1,0:T(8,128)(2,1)} %wq.1, ...), custom_call_target="tpu_custom_call" | custom-call | tf_op jit(solution)/shard_map/pallas_call | solution.py:860
  114.2 55.1 %shard_map.293 = (bf16[1032,768]{1,0:T(8,128)(2,1)}, f32[1032,768]{1,0:T(8,128)}, bf16[1032,768]{1,0:T(8,128)(2,1)}, bf16[768,768]{1,0:T(8,128)(2,1)}, f32[8,768...) custom-call(f32[1032,768]{1,0:T(8,128)} %get-tuple-element.48.tokens, ...), custom_call_target="tpu_custom_call" | custom-call | tf_op jit(solution)/shard_map/pallas_call | solution.py:1400
  169.2 76.4 %shard_map.294 = (bf16[1032,2304]{1,0:T(8,128)(2,1)}, f32[48,384]{1,0:T(8,128)}, f32[48,1536]{1,0:T(8,128)}, f32[192,384]{1,0:T(8,128)}, f32[16,768]{1,0:T(8,128)}) custom-call(s32[1]{0:T(128)S(6)} %copy.44.kind, bf16[18,1040,128]{2,1,0:T(8,128)(2,1)} %get-tuple-element.55.q_ref.k_ref.v_ref, bf16[18,1040,128]{2,1,0:T(8,128)(2,1)} %get-tuple-element.55.q_ref.k_ref.v_ref, ...), custom_call_target="tpu_custom_call" | custom-call | tf_op jit(solution)/shard_map/pallas_call | solution.py:1574
  245.7 71.8 %shard_map.295 = (f32[1560,128]{1,0:T(8,128)}, f32[128,128]{1,0:T(8,128)}, f32[1,128]{1,0:T(1,128)}, f32[48,1152]{1,0:T(8,128)}, f32[9,768]{1,0:T(8,128)}, /*ind...) custom-call(bf16[1032,2304]{1,0:T(8,128)(2,1)} %get-tuple-element.63.d_qkv, ...), custom_call_target="tpu_custom_call" | custom-call | tf_op jit(solution)/shard_map/pallas_call | solution.py:1270
  317.5 0.0 copy-start.5
  317.5 0.0 copy-start.9
  317.5 0.0 copy-start
  317.5 0.0 copy-start.6
  317.5 0.0 copy-start.3
  317.6 3.5 %copy.45 = f32[1024,640]{1,0:T(8,128)} copy(f32[1024,640]{1,0:T(8,128)} %get-tuple-element.97) | data formatting | bytes 5242880
  321.1 0.0 copy-done.5
  321.1 0.6 copy.46
  321.7 0.5 copy.47
  322.2 0.9 copy.48
  323.1 0.6 copy.49
  323.8 0.7 copy.50
  324.4 0.6 copy.51
  325.1 0.0 copy-done.2
  325.1 0.7 copy.52
  325.8 0.0 copy-done.1
  325.8 0.7 copy.53
  326.5 0.0 copy-done.7
  326.5 0.6 copy.54
  327.1 0.6 copy.55
  (11 shorter events, 0.0 us)
Async XLA Ops:
  317.5 3.6 %copy-start.5 = (f32[128,128]{1,0:T(8,128)S(1)}, f32[128,128]{1,0:T(8,128)}, u32[]{:S(2)}) copy-start(f32[128,128]{1,0:T(8,128)} %get-tuple-element.98) | copy-start | bytes 196612
  317.5 4.2 %copy-start.9 = (f32[1,128]{1,0:T(1,128)S(1)}, f32[1,128]{1,0:T(1,128)}, u32[]{:S(2)}) copy-start(f32[1,128]{1,0:T(1,128)} %get-tuple-element.75) | copy-start | bytes 1540
  317.5 4.7 %copy-start = (f32[1560,128]{1,0:T(8,128)S(1)}, f32[1560,128]{1,0:T(8,128)}, u32[]{:S(2)}) copy-start(f32[1560,128]{1,0:T(8,128)} %get-tuple-element.76) | copy-start | bytes 2396164
  317.5 5.6 %copy-start.6 = (f32[9,768]{1,0:T(8,128)S(1)}, f32[9,768]{1,0:T(8,128)}, u32[]{:S(2)}) copy-start(f32[9,768]{1,0:T(8,128)} %get-tuple-element.101) | copy-start | bytes 82948
  317.5 6.2 %copy-start.3 = (f32[48,1152]{1,0:T(8,128)S(1)}, f32[48,1152]{1,0:T(8,128)}, u32[]{:S(2)}) copy-start(f32[48,1152]{1,0:T(8,128)} %get-tuple-element.102) | copy-start | bytes 663556
  317.5 6.9 %copy-start.4 = (f32[48,384]{1,0:T(8,128)S(1)}, f32[48,384]{1,0:T(8,128)}, u32[]{:S(2)}) copy-start(f32[48,384]{1,0:T(8,128)} %get-tuple-element.103) | copy-start | bytes 221188
  317.5 7.5 %copy-start.2 = (f32[48,1536]{1,0:T(8,128)S(1)}, f32[48,1536]{1,0:T(8,128)}, u32[]{:S(2)}) copy-start(f32[48,1536]{1,0:T(8,128)} %get-tuple-element.104) | copy-start | bytes 884740
  317.6 8.2 %copy-start.1 = (f32[192,384]{1,0:T(8,128)S(1)}, f32[192,384]{1,0:T(8,128)}, u32[]{:S(2)}) copy-start(f32[192,384]{1,0:T(8,128)} %get-tuple-element.105) | copy-start | bytes 884740
  317.6 9.0 %copy-start.7 = (f32[6,48]{1,0:T(8,128)S(1)}, f32[6,48]{1,0:T(8,128)}, u32[]{:S(2)}) copy-start(f32[6,48]{1,0:T(8,128)} %get-tuple-element.82) | copy-start | bytes 3460
  317.6 9.5 %copy-start.8 = (f32[1,192]{1,0:T(1,128)S(1)}, f32[1,192]{1,0:T(1,128)}, u32[]{:S(2)}) copy-start(f32[1,192]{1,0:T(1,128)} %get-tuple-element.83) | copy-start | bytes 2308

commit v4 on v3

--- a/solution.py
+++ b/solution.py
@@ -741,6 +741,7 @@
     u.pass_on()
     d.send_z()
     e.send_z()
+    o.send_z()
     unpack(taken, flat, wide, kernel)
     bias = jnp.concatenate(
         [
@@ -802,7 +803,6 @@
         def _():
             d.pass_on()
             e.pass_on()
-            o.send_z()
 
         @pl.when(pair == 2)
         def _():

time: 328 us -> 329 us (level)
  no operation moved by 1% of the time
where the time goes in v4:
time: 329 us; the launch traced here: 328 us
  Pallas kernels  316 us (96%)
  local copies, waits for them, and re-layouts  10.1 us (3%)
    pallas_call x1, Pallas kernels, forward(): pl.pallas_call(forward_kernel, out_shape=outs, in_specs=[anywhere] * 4 +...  113 us
    pallas_call x1, Pallas kernels, attend_back(): pl.pallas_call(attend_back_kernel, grid=(HEADS // 2, 3), in_specs=[pl.Blo...  76.4 us
    pallas_call x1, Pallas kernels, closing(): pl.pallas_call(close_kernel, in_specs=[vmem] * len(operands) + [smem] * l...  71.8 us
    pallas_call x1, Pallas kernels, feed(): pl.pallas_call(feed_kernel, grid=(width // CHUNK,), in_specs=[block, bloc...  55.1 us
    unnamed x31, local copies, waits for them, and re-layouts  10.1 us

profile of v4, /device:TPU:0, one launch (start us, length us, event | category | flops | bytes accessed | tf_op | source)
XLA Modules:
  0.0 327.9 jit_solution(16104663849303729065)
XLA Ops:
  1.3 112.9 %shard_map.292 = (bf16[4,2,2,48,2304]{4,3,2,1,0:T(8,128)(2,1)}, bf16[4,2,2,48,768]{4,3,2,1,0:T(8,128)(2,1)}, bf16[4,2,2,48,3072]{4,3,2,1,0:T(8,128)(2,1)}, bf16[...) custom-call(bf16[48,1152]{1,0:T(8,128)(2,1)} %wq.1, ...), custom_call_target="tpu_custom_call" | custom-call | tf_op jit(solution)/shard_map/pallas_call | solution.py:860
  114.2 55.1 %shard_map.293 = (bf16[1032,768]{1,0:T(8,128)(2,1)}, f32[1032,768]{1,0:T(8,128)}, bf16[1032,768]{1,0:T(8,128)(2,1)}, bf16[768,768]{1,0:T(8,128)(2,1)}, f32[8,768...) custom-call(f32[1032,768]{1,0:T(8,128)} %get-tuple-element.48.tokens, ...), custom_call_target="tpu_custom_call" | custom-call | tf_op jit(solution)/shard_map/pallas_call | solution.py:1400
  169.2 76.4 %shard_map.294 = (bf16[1032,2304]{1,0:T(8,128)(2,1)}, f32[48,384]{1,0:T(8,128)}, f32[48,1536]{1,0:T(8,128)}, f32[192,384]{1,0:T(8,128)}, f32[16,768]{1,0:T(8,128)}) custom-call(s32[1]{0:T(128)S(6)} %copy.44.kind, bf16[18,1040,128]{2,1,0:T(8,128)(2,1)} %get-tuple-element.55.q_ref.k_ref.v_ref, bf16[18,1040,128]{2,1,0:T(8,128)(2,1)} %get-tuple-element.55.q_ref.k_ref.v_ref, ...), custom_call_target="tpu_custom_call" | custom-call | tf_op jit(solution)/shard_map/pallas_call | solution.py:1574
  245.7 71.8 %shard_map.295 = (f32[1560,128]{1,0:T(8,128)}, f32[128,128]{1,0:T(8,128)}, f32[1,128]{1,0:T(1,128)}, f32[48,1152]{1,0:T(8,128)}, f32[9,768]{1,0:T(8,128)}, /*ind...) custom-call(bf16[1032,2304]{1,0:T(8,128)(2,1)} %get-tuple-element.63.d_qkv, ...), custom_call_target="tpu_custom_call" | custom-call | tf_op jit(solution)/shard_map/pallas_call | solution.py:1270
  317.5 0.0 copy-start.5
  317.5 0.0 copy-start.9
  317.5 0.0 copy-start
  317.5 0.0 copy-start.6
  317.5 0.0 copy-start.3
  317.5 0.0 copy-start.4
  317.5 0.0 copy-start.2
  317.5 0.0 copy-start.1
  317.6 3.5 %copy.45 = f32[1024,640]{1,0:T(8,128)} copy(f32[1024,640]{1,0:T(8,128)} %get-tuple-element.97) | data formatting | bytes 5242880
  321.1 0.6 copy.46
  321.7 0.5 copy.47
  322.2 0.9 copy.48
  323.1 0.6 copy.49
  323.7 0.7 copy.50
  324.4 0.6 copy.51
  325.0 0.0 copy-done.2
  325.1 0.7 copy.52
  325.8 0.7 copy.53
  326.5 0.6 copy.54
  327.1 0.6 copy.55
  (11 shorter events, 0.0 us)
Async XLA Ops:
  317.5 3.6 %copy-start.5 = (f32[128,128]{1,0:T(8,128)S(1)}, f32[128,128]{1,0:T(8,128)}, u32[]{:S(2)}) copy-start(f32[128,128]{1,0:T(8,128)} %get-tuple-element.98) | copy-start | bytes 196612
  317.5 4.2 %copy-start.9 = (f32[1,128]{1,0:T(1,128)S(1)}, f32[1,128]{1,0:T(1,128)}, u32[]{:S(2)}) copy-start(f32[1,128]{1,0:T(1,128)} %get-tuple-element.75) | copy-start | bytes 1540
  317.5 4.7 %copy-start = (f32[1560,128]{1,0:T(8,128)S(1)}, f32[1560,128]{1,0:T(8,128)}, u32[]{:S(2)}) copy-start(f32[1560,128]{1,0:T(8,128)} %get-tuple-element.76) | copy-start | bytes 2396164
  317.5 5.6 %copy-start.6 = (f32[9,768]{1,0:T(8,128)S(1)}, f32[9,768]{1,0:T(8,128)}, u32[]{:S(2)}) copy-start(f32[9,768]{1,0:T(8,128)} %get-tuple-element.101) | copy-start | bytes 82948
  317.5 6.2 %copy-start.3 = (f32[48,1152]{1,0:T(8,128)S(1)}, f32[48,1152]{1,0:T(8,128)}, u32[]{:S(2)}) copy-start(f32[48,1152]{1,0:T(8,128)} %get-tuple-element.102) | copy-start | bytes 663556
  317.5 6.9 %copy-start.4 = (f32[48,384]{1,0:T(8,128)S(1)}, f32[48,384]{1,0:T(8,128)}, u32[]{:S(2)}) copy-start(f32[48,384]{1,0:T(8,128)} %get-tuple-element.103) | copy-start | bytes 221188
  317.5 7.5 %copy-start.2 = (f32[48,1536]{1,0:T(8,128)S(1)}, f32[48,1536]{1,0:T(8,128)}, u32[]{:S(2)}) copy-start(f32[48,1536]{1,0:T(8,128)} %get-tuple-element.104) | copy-start | bytes 884740
  317.5 8.2 %copy-start.1 = (f32[192,384]{1,0:T(8,128)S(1)}, f32[192,384]{1,0:T(8,128)}, u32[]{:S(2)}) copy-start(f32[192,384]{1,0:T(8,128)} %get-tuple-element.105) | copy-start | bytes 884740
  317.5 9.0 %copy-start.7 = (f32[6,48]{1,0:T(8,128)S(1)}, f32[6,48]{1,0:T(8,128)}, u32[]{:S(2)}) copy-start(f32[6,48]{1,0:T(8,128)} %get-tuple-element.82) | copy-start | bytes 3460
  317.5 9.5 %copy-start.8 = (f32[1,192]{1,0:T(1,128)S(1)}, f32[1,192]{1,0:T(1,128)}, u32[]{:S(2)}) copy-start(f32[1,192]{1,0:T(1,128)} %get-tuple-element.83) | copy-start | bytes 2308
